TPU v7x, 128 devices: a whole 4x4x4 slice. The times are simulated.
128 devices in a mesh: ab: 32 (over x, z, y_lo), cd: 4 (over y_hi, core).
Axes of the slice: x: 4, y: 4 (y_hi: 2, y_lo: 2; y = y_hi * 2 + y_lo), z: 4, core: 2. Of those that a mesh axis runs over, the one named last changes fastest.
Arguments:
- integrals: bfloat16 [96, 96, 128, 512], P('ab', None, None, 'cd'), may hold values from -0.0234375 to 0.0234375
- amplitudes: bfloat16 [16, 512, 512], P(None, 'ab', 'cd'), may hold values from -6 to 6
- block_sizes: int32 [4], replicated, may hold values from 1 to 128, 500 in all
Outputs:
- symmetric_residual: float32 [16, 96, 96], P(None, 'ab')
Inputs may be any that keep to these rules, and one draw needn't show every extreme that they name: `block_sizes`: the sizes sum to 500 and the largest is exactly 128.
All inputs are finite; a program needn't handle non-finite values.
Results may differ from a plain program's by a relative error of at most 0.0003.
Values may be sent and summed in bfloat16 or wider, within the bound.
A program may use at most 64 MiB of HBM per device.

v0:
```python
import jax
import jax.numpy as jnp
from jax import lax
from jax.sharding import PartitionSpec as P

IRREPS = 4
BLK = 128


def occupied_slots(block_sizes, first_slot, count):
    slot_ids = first_slot + jnp.arange(count, dtype=jnp.int32)
    irrep_ids = slot_ids // BLK
    owners = jnp.arange(IRREPS, dtype=jnp.int32)
    limits = jnp.sum(
        jnp.where(irrep_ids[:, None] == owners[None, :], block_sizes[None, :], 0), axis=1
    )
    return slot_ids % BLK < limits


def on_device(integrals, amplitudes, block_sizes):
    a_count = integrals.shape[0]
    window = integrals.shape[1]
    per_irrep = window // IRREPS
    c_rows = amplitudes.shape[1]
    own_block = lax.axis_index("cd")
    row_first = lax.axis_index("ab") * a_count
    keep_rows = occupied_slots(block_sizes, lax.axis_index("ab") * c_rows, c_rows)
    keep_cols = occupied_slots(block_sizes, own_block * BLK, BLK)
    keep_mask = keep_rows[:, None] & keep_cols[None, :]
    masked = jnp.where(keep_mask[None], amplitudes, jnp.zeros_like(amplitudes))
    panels = lax.all_gather(masked, "ab", axis=1, tiled=True)
    first_irrep = row_first // per_irrep
    pieces = []
    for second in range(IRREPS):
        source = jnp.bitwise_xor(jnp.bitwise_xor(first_irrep, second), own_block)
        amp_block = lax.dynamic_slice_in_dim(panels, source * BLK, BLK, 1)
        row_block = integrals[:, second * per_irrep : (second + 1) * per_irrep]
        pieces.append(
            jnp.einsum("abcd,pcd->pab", row_block, amp_block, preferred_element_type=jnp.float32)
        )
    partial_sum = jnp.concatenate(pieces, axis=2)
    ladder = lax.psum(partial_sum, "cd")
    mirrored = lax.all_to_all(ladder, "ab", split_axis=2, concat_axis=1, tiled=True)
    return ladder + jnp.transpose(mirrored, (0, 2, 1))


def solution(mesh):
    placed = (P("ab", None, None, "cd"), P(None, "ab", "cd"), P())
    return jax.shard_map(
        on_device, mesh=mesh, in_specs=placed, out_specs=P(None, "ab", None), check_vma=False
    )
```

profile of v0, /device:TPU:1, one launch (start us, length us, event | category | flops | bytes accessed | tf_op | source)
XLA Modules:
  0.0 215.1 jit_solution(4799325225221977902)
XLA Ops:
  6.5 0.0 all-gather.2.cloned.1.call-start
  6.5 0.7 select_reduce_fusion
  7.3 0.7 select_reduce_fusion.1
  8.1 0.1 broadcast_and_fusion
  8.2 1.5 copy_select_fusion
  9.6 0.0 all-gather.2.cloned.1.call-update
  9.7 7.4 %fusion.34 = (bf16[3,24,128,128]{3,2,1,0:T(8,128)(2,1)}, bf16[3,24,128,128]{3,2,1,0:T(8,128)(2,1)}, bf16[3,24,128,128]{3,2,1,0:T(8,128)(2,1)}, bf16[3,24,128,128]{3,2,1,0:T(8,128)(2,1)S(1)}) fusion(bf16[3,96,128,128]{3,2,1,0:T(8,128)(2,1)} %param.3), kind=kLoop, calls=%fused_computation.46 | loop fusion | bytes 18874368 | tf_op jit(solution)/shard_map/slice | solution.py:37
  17.1 128.5 %all-gather.2.cloned.1.call-done = bf16[16,512,128]{2,0,1:T(8,128)(2,1)} async-done(((bf16[16,16,128]{2,0,1:T(8,128)(2,1)}), bf16[16,512,128]{2,0,1:T(8,128)(2,1)}) %all-gather.2.cloned.1.call-update) | async-done | bytes 2097168 | tf_op jit(solution)/shard_map/all_gather | solution.py:31
  145.6 0.0 copy-start.1
  145.6 3.7 %fusion.11 = f32[16,3,24]{2,0,1:T(8,128)S(1)} fusion(bf16[3,24,128,128]{3,2,1,0:T(8,128)(2,1)} %get-tuple-element.7, bf16[16,512,128]{2,0,1:T(8,128)(2,1)} %all-gather.2.cloned.1.call-done, s32[]{:T(128)S(6)} %select_n.76), kind=kOutput, calls=%fused_computation.9 | convolution fusion | flops 37748736 | bytes 2888196 | tf_op jit(solution)/shard_map/abcd,pcd->pab/dot_general | solution.py:39
  149.3 0.0 copy-start
  149.3 0.0 copy-done.1
  149.3 3.0 %fusion.8 = f32[16,3,24]{2,0,1:T(8,128)S(1)} fusion(bf16[3,24,128,128]{3,2,1,0:T(8,128)(2,1)S(1)} %copy-done.1, bf16[16,512,128]{2,0,1:T(8,128)(2,1)} %all-gather.2.cloned.1.call-done, s32[]{:T(128)S(6)} %select_n.75), kind=kOutput, calls=%fused_computation.8 | convolution fusion | flops 37748736 | bytes 2888196 | tf_op jit(solution)/shard_map/abcd,pcd->pab/dot_general | solution.py:39
  152.3 0.0 copy-done
  152.3 2.8 %fusion.14 = f32[16,3,24]{2,0,1:T(8,128)S(1)} fusion(bf16[3,24,128,128]{3,2,1,0:T(8,128)(2,1)S(1)} %copy-done, bf16[16,512,128]{2,0,1:T(8,128)(2,1)} %all-gather.2.cloned.1.call-done, s32[]{:T(128)S(6)} %select_n.77), kind=kOutput, calls=%fused_computation.10 | convolution fusion | flops 37748736 | bytes 2888196 | tf_op jit(solution)/shard_map/abcd,pcd->pab/dot_general | solution.py:39
  155.1 2.8 %fusion.17 = f32[16,3,24]{2,0,1:T(8,128)S(1)} fusion(bf16[3,24,128,128]{3,2,1,0:T(8,128)(2,1)S(1)} %get-tuple-element.8, bf16[16,512,128]{2,0,1:T(8,128)(2,1)} %all-gather.2.cloned.1.call-done, s32[]{:T(128)S(6)} %select_n.78), kind=kOutput, calls=%fused_computation.11 | convolution fusion | flops 37748736 | bytes 2888196 | tf_op jit(solution)/shard_map/abcd,pcd->pab/dot_general | solution.py:39
  157.9 0.1 pad_maximum_fusion
  158.0 34.2 %psum.7 = f32[16,3,96]{2,0,1:T(8,128)S(1)} all-reduce(f32[16,3,96]{2,0,1:T(8,128)S(1)} %pad_maximum_fusion), channel_id=1, replica_groups=mesh['ab'=32,'cd'=4] {'cd'}, use_global_device_ids=true, to_apply=%region_2.3 | all-reduce | flops 4608 | bytes 36864 | tf_op jit(solution)/shard_map/psum | solution.py:42
  192.2 0.1 copy.32
  192.3 0.2 reshape.108
  192.5 13.5 %all_to_all.18 = f32[32,1,144]{2,1,0:T(1,128)S(1)} all-to-all(f32[32,1,144]{2,1,0:T(1,128)S(1)} %reshape.108), channel_id=1, replica_groups=mesh['ab'=32,'cd'=4] {'ab'}, dimensions={0} | all-to-all | bytes 36864 | tf_op jit(solution)/shard_map/all_to_all | solution.py:43
  206.0 0.5 broadcast.182
  206.5 0.7 reduce
  207.3 0.1 reshape.109
  207.5 0.1 all_to_all.16
  207.5 0.1 copy.35
  207.6 0.6 bitcast_add_fusion
  (5 shorter events, 0.1 us)
Async XLA Ops:
  6.5 139.1 %all-gather.2.cloned.1.call-start = ((), (), s32[]{:S(2)}) async-start(), calls=%async_computation.1 | async-start | bytes 2162688 | tf_op jit(solution)/shard_map/all_gather | solution.py:31
  145.6 3.7 %copy-start.1 = (bf16[3,24,128,128]{3,2,1,0:T(8,128)(2,1)S(1)}, bf16[3,24,128,128]{3,2,1,0:T(8,128)(2,1)}, u32[]{:S(2)}) copy-start(bf16[3,24,128,128]{3,2,1,0:T(8,128)(2,1)} %get-tuple-element.5) | copy-start | bytes 7077892
  149.3 3.0 %copy-start = (bf16[3,24,128,128]{3,2,1,0:T(8,128)(2,1)S(1)}, bf16[3,24,128,128]{3,2,1,0:T(8,128)(2,1)}, u32[]{:S(2)}) copy-start(bf16[3,24,128,128]{3,2,1,0:T(8,128)(2,1)} %get-tuple-element.6) | copy-start | bytes 7077892
Sparse Core Ops, SparseCore 0:
  9.8 135.7 all-gather.1
where the time goes:
time: 216 us; the launch traced here: 215 us
  waiting for transfers between devices  129 us (60%)
  blocking collectives  47.7 us (22%)
  between operations  13.5 us (6%)
  matrix products  12.3 us (6%)
  local copies, waits for them, and re-layouts  8.51 us (4%)
  other arithmetic  4.54 us (2%)
    all_gather x1, waiting for transfers between devices, on_device(): panels = lax.all_gather(masked, 'ab', axis=1, tiled=True)  129 us
    psum x1, blocking collectives, on_device(): ladder = lax.psum(partial_sum, 'cd')  34.2 us
    all_to_all x1, blocking collectives, on_device(): lax.all_to_all(ladder, 'ab', split_axis=2, concat_axis=1, tiled=True)  13.5 us
    dot_general x4, matrix products, on_device(): jnp.einsum('abcd,pcd->pab', row_block, amp_block, preferred_element_type=...  12.3 us
    slice x1, local copies, waits for them, and re-layouts, on_device(): row_block = integrals[:, second * per_irrep:(second + 1) * per_irrep]  7.4 us
  transfers between devices with their start and end apart: 1, of which 1 were waited for; matrix products, arithmetic and copies ran while one was open for 3% of the time, Pallas kernels for 0%

commit v1 on v0

v1 whole, which is shorter than its diff:
```python
import jax
import jax.numpy as jnp
from jax import lax
from jax.experimental import pallas as pl
from jax.experimental.pallas import tpu as pltpu
from jax.sharding import PartitionSpec as P

IRREPS = 4
BLK = 128
NPAIR = 16
WIR = 24
GROUP = 8
OWN = 3
CB = 16
MESH = pl.DeviceIdType.MESH
F32 = jnp.float32
BF16 = jnp.bfloat16


def iota(shape, dim):
    return lax.broadcasted_iota(jnp.int32, shape, dim)


def split3(x, axis):
    high = x.astype(BF16)
    rest = x - high.astype(F32)
    middle = rest.astype(BF16)
    low = (rest - middle.astype(F32)).astype(BF16)
    return jnp.concatenate([high, middle, low], axis=axis)


def kernel(
    sizes, amps, integrals, out, ints, panels, acc, own, msgs, mirror, shares,
    ints_sem, amp_send, amp_recv, msg_send, msg_recv, share_send, share_recv,
):
    ab = lax.axis_index("ab")
    cd = lax.axis_index("cd")
    irrep = ab // GROUP
    slot = lax.rem(ab, GROUP)
    slot_low = lax.rem(slot // 2, 2)
    slot_lane = lax.rem(slot, 2)

    fetch = pltpu.make_async_copy(integrals, ints, ints_sem)
    fetch.start()

    barrier = pltpu.get_barrier_semaphore()

    def greet(i, carry):
        pl.semaphore_signal(
            barrier, inc=1, device_id=(lax.rem(ab + i, 32), cd), device_id_type=MESH
        )
        return carry

    lax.fori_loop(1, 32, greet, 0)
    for i in range(1, 4):
        pl.semaphore_signal(barrier, inc=1, device_id=(ab, lax.rem(cd + i, 4)), device_id_type=MESH)

    row_limit = sizes[irrep] - slot * CB
    col_limit = sizes[cd]
    shape = (NPAIR * CB, BLK)
    keep = (lax.rem(iota(shape, 0), CB) < row_limit) & (iota(shape, 1) < col_limit)
    plain = amps[...].reshape(shape).astype(F32)
    panels[ab] = jnp.where(keep, plain, 0.0).T.astype(BF16)

    pl.semaphore_wait(barrier, 34)

    def amp_copy(i, peer, block):
        return pltpu.make_async_remote_copy(
            src_ref=panels.at[block],
            dst_ref=panels.at[block],
            send_sem=amp_send.at[i],
            recv_sem=amp_recv.at[block],
            device_id=(peer, cd),
            device_id_type=MESH,
        )

    def spread(i, carry):
        amp_copy(i, ab ^ i, ab).start()
        return carry

    lax.fori_loop(1, 32, spread, 0)
    fetch.wait()

    low_half = lax.rem(iota((8, 256), 1), 16) < 8
    diagonal = lax.rem(iota((8, 256), 1), 8) == iota((8, 256), 0)
    spread_pairs = (
        lax.rem(iota((768, 128), 1), 16) == lax.rem(iota((768, 128), 0), 256) // CB
    ).astype(BF16)
    row = iota((72, 128), 0)
    lane = iota((72, 128), 1)
    lane_slot, lane_item = lane // 64, lax.rem(lane, 64) // 16
    row_a, row_b = row // WIR, lax.rem(row, WIR)
    own_keep = (lane_slot == lax.rem(row_b // OWN, 2)) & (lane_item == lax.rem(row_b, OWN))
    msg_keep = (lane_slot == slot_lane) & (lane_item == row_a)
    to = iota((80, 144), 0)
    frm = iota((80, 144), 1)
    frm_row = lax.rem(frm, 72)
    frm_a, frm_b = frm_row // WIR, lax.rem(frm_row, WIR)
    frm_slot, frm_k = frm_b // OWN, lax.rem(frm_b, OWN)
    place = jnp.where(
        frm < 72,
        (frm_slot // 4) * 8 + lax.rem(frm_slot // 2, 2) * 4 + frm_a,
        16 + frm_slot * 8 + slot_low * 4 + frm_k,
    )
    gather_rows = (to == place).astype(BF16)
    gather_rows = jnp.concatenate([gather_rows] * 3, axis=1)

    def msg_copy(peer, block, sender):
        return pltpu.make_async_remote_copy(
            src_ref=msgs.at[block],
            dst_ref=mirror.at[sender],
            send_sem=msg_send.at[block],
            recv_sem=msg_recv.at[sender],
            device_id=(peer, cd),
            device_id_type=MESH,
        )

    def panel(step, carry):
        rel = step ^ (step // 2)
        source = irrep ^ rel
        second = source ^ irrep ^ cd

        def pair(t, inner):
            for j in range(2):
                block = source * GROUP + 2 * t + j

                @pl.when(block != ab)
                def _():
                    amp_copy(0, ab, block).wait_recv()

            first_block = source * GROUP + 2 * t
            weights = panels[pl.ds(first_block, 2)].reshape(256, 256)
            first_c = pl.multiple_of(2 * t * CB, 2 * CB)
            for a in range(OWN):
                rows = ints[a, pl.ds(second * WIR, WIR), pl.ds(first_c, 2 * CB), :]
                left = jnp.concatenate([rows[:, :CB], rows[:, CB:]], axis=2).reshape(WIR * CB, 256)
                term = jnp.dot(left, weights, preferred_element_type=F32)
                term = term.reshape(WIR, 2, 8, 256)
                term = jnp.where(low_half[None], term[:, 0], term[:, 1])
                here = pl.ds(a * WIR, WIR)
                acc[here] = jnp.where(t == 0, term, acc[here] + term)
            return inner

        lax.fori_loop(0, 4, pair, 0)
        folded = jnp.sum(jnp.where(diagonal[None], acc[...], 0.0), axis=1)
        values = jnp.dot(split3(folded, 1), spread_pairs, preferred_element_type=F32)
        both = jnp.concatenate(
            [jnp.where(own_keep, values, 0.0), jnp.where(msg_keep, values, 0.0)], axis=0
        )
        placed = jnp.dot(gather_rows, split3(both, 0), preferred_element_type=F32)
        own[second] = placed[:16].reshape(2, 8, 128)
        msgs[pl.ds(second * GROUP, GROUP)] = placed[16:].reshape(GROUP, 8, 128)

        def send(i, inner):
            peer = second * GROUP + i

            @pl.when(peer != ab)
            def _():
                msg_copy(peer, peer, ab).start()

            return inner

        lax.fori_loop(0, GROUP, send, 0)
        return carry

    lax.fori_loop(0, IRREPS, panel, 0)
    mirror[ab] = msgs[ab]

    def collect(i, carry):
        msg_copy(ab, ab, ab ^ i).wait_recv()
        return carry

    lax.fori_loop(1, 32, collect, 0)
    total = own[...] + jnp.sum(mirror[...].reshape(IRREPS, 2, 4, 8, 128), axis=2)
    shares[cd] = total

    def share_copy(i, peer, sender):
        return pltpu.make_async_remote_copy(
            src_ref=shares.at[sender],
            dst_ref=shares.at[sender],
            send_sem=share_send.at[i],
            recv_sem=share_recv.at[sender],
            device_id=(ab, peer),
            device_id_type=MESH,
        )

    for i in range(1, 4):
        share_copy(i, cd ^ i, cd).start()
    for i in range(1, 4):
        share_copy(i, cd, cd ^ i).wait_recv()
    out[...] = (shares[0] + shares[1]) + (shares[2] + shares[3])

    def finish(i, carry):
        amp_copy(i, ab, ab).wait_send()
        msg_copy(ab, ab ^ i, ab).wait_send()
        return carry

    lax.fori_loop(1, 32, finish, 0)
    for i in range(1, 4):
        share_copy(i, cd, cd).wait_send()


def on_device(integrals, amplitudes, block_sizes):
    vmem = pl.BlockSpec(memory_space=pltpu.VMEM)
    packed = pl.pallas_call(
        kernel,
        out_shape=jax.ShapeDtypeStruct((IRREPS, 2, 8, 128), F32),
        in_specs=[
            pl.BlockSpec(memory_space=pltpu.SMEM),
            vmem,
            pl.BlockSpec(memory_space=pl.ANY),
        ],
        out_specs=vmem,
        scratch_shapes=[
            pltpu.VMEM(integrals.shape, BF16),
            pltpu.VMEM((32, BLK, NPAIR * CB), BF16),
            pltpu.VMEM((OWN * WIR, 8, 256), F32),
            pltpu.VMEM((IRREPS, 2, 8, 128), F32),
            pltpu.VMEM((32, 8, 128), F32),
            pltpu.VMEM((32, 8, 128), F32),
            pltpu.VMEM((4, IRREPS, 2, 8, 128), F32),
            pltpu.SemaphoreType.DMA,
            pltpu.SemaphoreType.DMA((32,)),
            pltpu.SemaphoreType.DMA((32,)),
            pltpu.SemaphoreType.DMA((32,)),
            pltpu.SemaphoreType.DMA((32,)),
            pltpu.SemaphoreType.DMA((4,)),
            pltpu.SemaphoreType.DMA((4,)),
        ],
        compiler_params=pltpu.CompilerParams(
            collective_id=0, has_side_effects=True, vmem_limit_bytes=56 << 20
        ),
        name="ladder",
    )(block_sizes, amplitudes, integrals)
    packed = packed.reshape(IRREPS, 2, 2, 4, 2, 4, NPAIR)[:, :, :, :OWN, :, :OWN]
    return packed.transpose(6, 3, 0, 1, 2, 4, 5).reshape(NPAIR, OWN, IRREPS * WIR)


def solution(mesh):
    placed = (P("ab", None, None, "cd"), P(None, "ab", "cd"), P())
    return jax.shard_map(
        on_device, mesh=mesh, in_specs=placed, out_specs=P(None, "ab", None), check_vma=False
    )
```

time: 216 us -> 62.8 us (0.29)
  waiting for transfers between devices: 129 us -> 0 us
  Pallas kernels: 0 us -> 60.8 us
  blocking collectives: 47.7 us -> 0 us
  between operations: 13.5 us -> 0.03 us
  matrix products: 12.3 us -> 0 us
  local copies, waits for them, and re-layouts: 8.51 us -> 1.76 us
  other arithmetic: 4.54 us -> 0 us
    all_gather x1 -> x0, waiting for transfers between devices: 129 us -> none  [on_device(): panels = lax.all_gather(masked, 'ab', axis=1, tiled=True)]
    pallas_call x0 -> x1, Pallas kernels: none -> 60.8 us  [on_device(): pl.pallas_call(kernel, out_shape=jax.ShapeDtypeStruct((IRREPS, 2, 8, 128)...]
    psum x1 -> x0, blocking collectives: 34.2 us -> none  [on_device(): ladder = lax.psum(partial_sum, 'cd')]
    all_to_all x1 -> x0, blocking collectives: 13.5 us -> none  [on_device(): lax.all_to_all(ladder, 'ab', split_axis=2, concat_axis=1, tiled=True)]
    dot_general x4 -> x0, matrix products: 12.3 us -> none  [on_device(): jnp.einsum('abcd,pcd->pab', row_block, amp_block, preferred_element_type=...]
    slice x1 -> x0, local copies, waits for them, and re-layouts: 7.4 us -> none  [on_device(): row_block = integrals[:, second * per_irrep:(second + 1) * per_irrep]]
  transfers between devices with their start and end apart: 1 -> 0, of which waited for: 1 -> 0; matrix products, arithmetic and copies ran while one was open for 3% -> 0% of each run, Pallas kernels for 0% -> 0%
where the time goes in v1:
time: 62.8 us; the launch traced here: 62.6 us
  Pallas kernels  60.8 us (97%)
  local copies, waits for them, and re-layouts  1.76 us (3%)
    pallas_call x1, Pallas kernels, on_device(): pl.pallas_call(kernel, out_shape=jax.ShapeDtypeStruct((IRREPS, 2, 8, 128)...  60.8 us

profile of v1, /device:TPU:1, one launch (start us, length us, event | category | flops | bytes accessed | tf_op | source)
XLA Modules:
  0.0 62.6 jit_solution(4983665302093614527)
XLA Ops:
  0.0 60.8 %ladder.1 = f32[4,2,8,128]{3,2,1,0:T(8,128)} custom-call(s32[4]{0:T(128)} %sizes.1, bf16[16,16,128]{2,1,0:T(8,128)(2,1)} %amps.1, bf16[3,96,128,128]{3,2,1,0:T(8,128)(2,1)} %integrals.1), custom_call_target="tpu_custom_call" | custom-call | tf_op jit(solution)/shard_map/ladder/pallas_call | solution.py:205
  60.8 1.0 %reshape.6 = f32[4,2,2,4,2,4,16]{6,5,4,3,2,1,0:T(4,128)S(1)} reshape(f32[4,2,8,128]{3,2,1,0:T(8,128)} %ladder.1) | data formatting | bytes 65536 | tf_op jit(solution)/shard_map/reshape | solution.py:235
  61.8 0.1 reshape.7
  61.9 0.7 %copy.6 = f32[16,3,96]{2,0,1:T(8,128)} copy(f32[16,3,96]{0,2,1:T(8,128)S(1)} %reshape.7) | data formatting | bytes 36864 | tf_op jit(solution)/shard_map/reshape | solution.py:236
  (1 shorter events, 0.0 us)

commit v2 on v1

v2 whole, which is shorter than its diff:
```python
import jax
import jax.numpy as jnp
from jax import lax
from jax.experimental import pallas as pl
from jax.experimental.pallas import tpu as pltpu
from jax.sharding import PartitionSpec as P

IRREPS = 4
BLK = 128
NPAIR = 16
WIR = 24
GROUP = 8
OWN = 3
CB = 16
MESH = pl.DeviceIdType.MESH
F32 = jnp.float32
BF16 = jnp.bfloat16


def iota(shape, dim):
    return lax.broadcasted_iota(jnp.int32, shape, dim)


def split3(x, axis):
    high = x.astype(BF16)
    rest = x - high.astype(F32)
    middle = rest.astype(BF16)
    low = (rest - middle.astype(F32)).astype(BF16)
    return jnp.concatenate([high, middle, low], axis=axis)


def kernel(
    sizes, amps, integrals, out, ints, plain, panels, acc, own, msgs, mirror, shares,
    ints_sem, plain_sem, send_sem, item_recv, pair_recv, msg_send, msg_recv, share_send, share_recv,
):
    ab = lax.axis_index("ab")
    cd = lax.axis_index("cd")
    irrep = ab // GROUP
    slot = lax.rem(ab, GROUP)
    slot_low = lax.rem(slot // 2, 2)
    slot_lane = lax.rem(slot, 2)
    ring = slot // 2
    pick = slot_lane

    fetch_own = pltpu.make_async_copy(amps, plain, plain_sem)
    fetch_own.start()

    def place(half, du, dv, y):
        if half == 0:
            return lax.rem(irrep + dv, 4) * GROUP + lax.rem(ring + du, 4) * 2 + y
        return lax.rem(irrep + du, 4) * GROUP + lax.rem(ring + dv, 4) * 2 + y

    plane = [(0, 1), (1, 0), (3, 0), (1, 1), (3, 1), (2, 0), (2, 1)]

    def peer_of(half, du, dy):
        return place(half, du, 0, lax.rem(pick + dy, 2))

    barrier = pltpu.get_barrier_semaphore()
    for half in range(2):
        for du, dy in plane[half:]:
            pl.semaphore_signal(
                barrier, inc=1, device_id=(peer_of(half, du, dy), cd), device_id_type=MESH
            )
    for i in range(1, 4):
        pl.semaphore_signal(barrier, inc=1, device_id=(ab, cd ^ i), device_id_type=MESH)

    fetch = pltpu.make_async_copy(integrals, ints, ints_sem)
    fetch.start()

    row_limit = sizes[irrep] - slot * CB
    col_limit = sizes[cd]
    shape = (NPAIR * CB, BLK)
    keep = (lax.rem(iota(shape, 0), CB) < row_limit) & (iota(shape, 1) < col_limit)
    fetch_own.wait()
    turned = jnp.where(keep, plain[...].reshape(shape).astype(F32), 0.0).T.astype(BF16)
    panels[0, ab] = turned[:, :128]
    panels[1, ab] = turned[:, 128:]

    def item_copy(i, half, peer, block):
        return pltpu.make_async_remote_copy(
            src_ref=panels.at[half, block],
            dst_ref=panels.at[half, block],
            send_sem=send_sem.at[i],
            recv_sem=item_recv.at[half, block],
            device_id=(peer, cd),
            device_id_type=MESH,
        )

    def pair_copy(i, half, peer, first):
        return pltpu.make_async_remote_copy(
            src_ref=panels.at[half, pl.ds(first, 2)],
            dst_ref=panels.at[half, pl.ds(first, 2)],
            send_sem=send_sem.at[i],
            recv_sem=pair_recv.at[half, first // 2],
            device_id=(peer, cd),
            device_id_type=MESH,
        )

    def item_arrived(half, du, y):
        item_copy(0, half, ab, place(half, du, 0, y)).wait_recv()

    def pair_arrived(half, du, dv):
        pair_copy(0, half, ab, place(half, du, dv, 0)).wait_recv()

    def forward(i, half, du, dv, to):
        pair_copy(i, half, place(half, 0, to, pick), place(half, du, dv, 0)).start()

    pl.semaphore_wait(barrier, 16)

    for n, (du, dy) in enumerate(plane):
        for half in range(2):
            item_copy(2 * n + half, half, peer_of(half, du, dy), ab).start()

    acc[...] = jnp.zeros_like(acc)

    for half in range(2):
        item_arrived(half, 0, 1 - pick)
        forward(14 + 2 * half, half, 0, 0, 1)
        forward(15 + 2 * half, half, 0, 0, 3)
    for n, du in enumerate((1, 3, 2)):
        for half in range(2):
            item_arrived(half, du, 0)
            item_arrived(half, du, 1)
            forward(18 + 4 * n + 2 * half, half, du, 0, 1)
            forward(19 + 4 * n + 2 * half, half, du, 0, 3)

    low_half = lax.rem(iota((8, 256), 1), 16) < 8

    def tile(dx, dz):
        source = lax.rem(irrep + dx, 4)
        second = source ^ irrep ^ cd
        at = lax.rem(ring + dz, 4)
        first = source * GROUP + at * 2
        weights = jnp.concatenate(
            [panels[half, pl.ds(first, 2)].reshape(256, 128) for half in range(2)], axis=1
        )
        first_c = pl.multiple_of(at * 2 * CB, 2 * CB)
        rows = ints[:, pl.ds(second * WIR, WIR), pl.ds(first_c, 2 * CB), :]
        left = jnp.concatenate([rows[:, :, :CB], rows[:, :, CB:]], axis=3)
        left = left.reshape(OWN * WIR * CB, 256)
        term = jnp.dot(left, weights, preferred_element_type=F32)
        term = term.reshape(OWN * WIR, 2, 8, 256)
        acc[second] += jnp.where(low_half[None], term[:, 0], term[:, 1])

    def tiles(count, dx_of, dz_of):
        def body(i, carry):
            tile(dx_of(i), dz_of(i))
            return carry

        lax.fori_loop(0, count, body, 0)

    relays = [(0, 3, 1), (1, 1, 3), (3, 1, 3), (2, 3, 1)]

    def relay(n):
        du, dv, to = relays[n]
        for half in range(2):
            pair_arrived(half, du, dv)
            forward(30 + 2 * n + half, half, du, dv, to)

    relay(0)
    fetch.wait()
    tile(0, 0)
    relay(1)
    relay(2)
    for half in range(2):
        pair_arrived(half, 0, 1)
    tiles(4, lambda i: lax.rem(i // 2 * (2 * i + 1), 4), lambda i: (1 - i // 2) * (2 * i + 1))
    relay(3)
    for half in range(2):
        for du in (1, 3):
            pair_arrived(half, du, 3)
        pair_arrived(half, 2, 1)
    tiles(4, lambda i: i // 2 * 2 + 1, lambda i: lax.rem(i, 2) * 2 + 1)

    diagonal = lax.rem(iota((8, 256), 1), 8) == iota((8, 256), 0)
    spread_pairs = (
        lax.rem(iota((768, 128), 1), 16) == lax.rem(iota((768, 128), 0), 256) // CB
    ).astype(BF16)
    row = iota((72, 128), 0)
    lane = iota((72, 128), 1)
    lane_slot, lane_item = lane // 64, lax.rem(lane, 64) // 16
    row_a, row_b = row // WIR, lax.rem(row, WIR)
    own_keep = (lane_slot == lax.rem(row_b // OWN, 2)) & (lane_item == lax.rem(row_b, OWN))
    msg_keep = (lane_slot == slot_lane) & (lane_item == row_a)
    to = iota((80, 144), 0)
    frm = iota((80, 144), 1)
    frm_row = lax.rem(frm, 72)
    frm_a, frm_b = frm_row // WIR, lax.rem(frm_row, WIR)
    frm_slot, frm_k = frm_b // OWN, lax.rem(frm_b, OWN)
    goal = jnp.where(
        frm < 72,
        (frm_slot // 4) * 8 + lax.rem(frm_slot // 2, 2) * 4 + frm_a,
        16 + frm_slot * 8 + slot_low * 4 + frm_k,
    )
    gather_rows = (to == goal).astype(BF16)
    gather_rows = jnp.concatenate([gather_rows] * 3, axis=1)

    def msg_copy(peer, block, sender):
        return pltpu.make_async_remote_copy(
            src_ref=msgs.at[block],
            dst_ref=mirror.at[sender],
            send_sem=msg_send.at[block],
            recv_sem=msg_recv.at[sender],
            device_id=(peer, cd),
            device_id_type=MESH,
        )

    def finish(dx):
        second = lax.rem(irrep + dx, 4) ^ irrep ^ cd
        folded = jnp.sum(jnp.where(diagonal[None], acc[second], 0.0), axis=1)
        values = jnp.dot(split3(folded, 1), spread_pairs, preferred_element_type=F32)
        both = jnp.concatenate(
            [jnp.where(own_keep, values, 0.0), jnp.where(msg_keep, values, 0.0)], axis=0
        )
        placed = jnp.dot(gather_rows, split3(both, 0), preferred_element_type=F32)
        own[second] = placed[:16].reshape(2, 8, 128)
        msgs[pl.ds(second * GROUP, GROUP)] = placed[16:].reshape(GROUP, 8, 128)

        def send(i, inner):
            peer = second * GROUP + i

            @pl.when(peer != ab)
            def _():
                msg_copy(peer, peer, ab).start()

            return inner

        lax.fori_loop(0, GROUP, send, 0)

    for half in range(2):
        pair_arrived(half, 0, 2)
    tile(0, 2)
    finish(0)
    for half in range(2):
        for du in (1, 3):
            pair_arrived(half, du, 2)
        pair_arrived(half, 2, 2)

    def rest(i, carry):
        dx = 2 * i + 1
        tile(dx, 2)
        finish(dx)
        return carry

    lax.fori_loop(0, 2, rest, 0)
    tiles(4, lambda i: 2, lambda i: i)
    finish(2)
    mirror[ab] = msgs[ab]

    def collect(i, carry):
        msg_copy(ab, ab, ab ^ i).wait_recv()
        return carry

    lax.fori_loop(1, 32, collect, 0)
    total = own[...] + jnp.sum(mirror[...].reshape(IRREPS, 2, 4, 8, 128), axis=2)
    shares[cd] = total

    def share_copy(i, peer, sender):
        return pltpu.make_async_remote_copy(
            src_ref=shares.at[sender],
            dst_ref=shares.at[sender],
            send_sem=share_send.at[i],
            recv_sem=share_recv.at[sender],
            device_id=(ab, peer),
            device_id_type=MESH,
        )

    for i in range(1, 4):
        share_copy(i, cd ^ i, cd).start()
    for i in range(1, 4):
        share_copy(i, cd, cd ^ i).wait_recv()
    out[...] = (shares[0] + shares[1]) + (shares[2] + shares[3])

    def sent_items(i, carry):
        item_copy(i, 0, ab, ab).wait_send()
        return carry

    def sent_pairs(i, carry):
        pair_copy(i, 0, ab, 0).wait_send()
        return carry

    def sent_msgs(i, carry):
        msg_copy(ab, ab ^ i, ab).wait_send()
        return carry

    lax.fori_loop(0, 14, sent_items, 0)
    lax.fori_loop(14, 38, sent_pairs, 0)
    lax.fori_loop(1, 32, sent_msgs, 0)
    for i in range(1, 4):
        share_copy(i, cd, cd).wait_send()


def on_device(integrals, amplitudes, block_sizes):
    vmem = pl.BlockSpec(memory_space=pltpu.VMEM)
    packed = pl.pallas_call(
        kernel,
        out_shape=jax.ShapeDtypeStruct((IRREPS, 2, 8, 128), F32),
        in_specs=[
            pl.BlockSpec(memory_space=pltpu.SMEM),
            pl.BlockSpec(memory_space=pl.ANY),
            pl.BlockSpec(memory_space=pl.ANY),
        ],
        out_specs=vmem,
        scratch_shapes=[
            pltpu.VMEM(integrals.shape, BF16),
            pltpu.VMEM(amplitudes.shape, BF16),
            pltpu.VMEM((2, 32, BLK, NPAIR * CB // 2), BF16),
            pltpu.VMEM((IRREPS, OWN * WIR, 8, 256), F32),
            pltpu.VMEM((IRREPS, 2, 8, 128), F32),
            pltpu.VMEM((32, 8, 128), F32),
            pltpu.VMEM((32, 8, 128), F32),
            pltpu.VMEM((4, IRREPS, 2, 8, 128), F32),
            pltpu.SemaphoreType.DMA,
            pltpu.SemaphoreType.DMA,
            pltpu.SemaphoreType.DMA((38,)),
            pltpu.SemaphoreType.DMA((2, 32)),
            pltpu.SemaphoreType.DMA((2, 16)),
            pltpu.SemaphoreType.DMA((32,)),
            pltpu.SemaphoreType.DMA((32,)),
            pltpu.SemaphoreType.DMA((4,)),
            pltpu.SemaphoreType.DMA((4,)),
        ],
        compiler_params=pltpu.CompilerParams(
            collective_id=0, has_side_effects=True, vmem_limit_bytes=56 << 20
        ),
        name="ladder",
    )(block_sizes, amplitudes, integrals)
    packed = packed.reshape(IRREPS, 2, 2, 4, 2, 4, NPAIR)[:, :, :, :OWN, :, :OWN]
    return packed.transpose(6, 3, 0, 1, 2, 4, 5).reshape(NPAIR, OWN, IRREPS * WIR)


def solution(mesh):
    placed = (P("ab", None, None, "cd"), P(None, "ab", "cd"), P())
    return jax.shard_map(
        on_device, mesh=mesh, in_specs=placed, out_specs=P(None, "ab", None), check_vma=False
    )
```

time: 62.8 us -> 45.8 us (0.73)
  Pallas kernels: 60.8 us -> 43.8 us
    pallas_call x1, Pallas kernels: 60.8 us -> 43.8 us  [on_device(): pl.pallas_call(kernel, out_shape=jax.ShapeDtypeStruct((IRREPS, 2, 8, 128)...]
where the time goes in v2:
time: 45.8 us; the launch traced here: 45.6 us
  Pallas kernels  43.8 us (96%)
  local copies, waits for them, and re-layouts  1.76 us (4%)
    pallas_call x1, Pallas kernels, on_device(): pl.pallas_call(kernel, out_shape=jax.ShapeDtypeStruct((IRREPS, 2, 8, 128)...  43.8 us
    reshape x1, local copies, waits for them, and re-layouts, on_device(): packed.reshape(IRREPS, 2, 2, 4, 2, 4, NPAIR)[:, :, :, :OWN, :, :OWN]  0.97 us

profile of v2, /device:TPU:1, one launch (start us, length us, event | category | flops | bytes accessed | tf_op | source)
XLA Modules:
  0.0 45.6 jit_solution(18441558846844827004)
XLA Ops:
  0.0 43.8 %ladder.1 = f32[4,2,8,128]{3,2,1,0:T(8,128)} custom-call(s32[4]{0:T(128)} %sizes.1, bf16[16,16,128]{2,1,0:T(8,128)(2,1)} %amps.1, bf16[3,96,128,128]{3,2,1,0:T(8,128)(2,1)} %integrals.1), custom_call_target="tpu_custom_call" | custom-call | tf_op jit(solution)/shard_map/ladder/pallas_call | solution.py:295
  43.8 1.0 %reshape.6 = f32[4,2,2,4,2,4,16]{6,5,4,3,2,1,0:T(4,128)S(1)} reshape(f32[4,2,8,128]{3,2,1,0:T(8,128)} %ladder.1) | data formatting | bytes 65536 | tf_op jit(solution)/shard_map/reshape | solution.py:328
  44.8 0.1 reshape.7
  44.9 0.7 %copy.6 = f32[16,3,96]{2,0,1:T(8,128)} copy(f32[16,3,96]{0,2,1:T(8,128)S(1)} %reshape.7) | data formatting | bytes 36864 | tf_op jit(solution)/shard_map/reshape | solution.py:329
  (1 shorter events, 0.0 us)

commit v3 on v2

--- a/solution.py
+++ b/solution.py
@@ -21,17 +21,16 @@
     return lax.broadcasted_iota(jnp.int32, shape, dim)
 
 
-def split3(x, axis):
+def split2(x, axis):
     high = x.astype(BF16)
-    rest = x - high.astype(F32)
-    middle = rest.astype(BF16)
-    low = (rest - middle.astype(F32)).astype(BF16)
-    return jnp.concatenate([high, middle, low], axis=axis)
+    low = (x - high.astype(F32)).astype(BF16)
+    return jnp.concatenate([high, low], axis=axis)
 
 
 def kernel(
-    sizes, amps, integrals, out, ints, plain, panels, acc, own, msgs, mirror, shares,
-    ints_sem, plain_sem, send_sem, item_recv, pair_recv, msg_send, msg_recv, share_send, share_recv,
+    sizes, amps, integrals, out, ints, plain, panels, acc, msgs, mirror, shares, lates,
+    ints_sem, plain_sem, send_sem, item_recv, pair_recv, msg_send, msg_recv,
+    share_send, share_recv, late_send, late_recv, token,
 ):
     ab = lax.axis_index("ab")
     cd = lax.axis_index("cd")
@@ -41,6 +40,8 @@
     slot_lane = lax.rem(slot, 2)
     ring = slot // 2
     pick = slot_lane
+    core = lax.rem(cd, 2)
+    late = cd ^ 2
 
     fetch_own = pltpu.make_async_copy(amps, plain, plain_sem)
     fetch_own.start()
@@ -112,6 +113,7 @@
             item_copy(2 * n + half, half, peer_of(half, du, dy), ab).start()
 
     acc[...] = jnp.zeros_like(acc)
+    shares[cd, late] = jnp.zeros((2, 8, 128), F32)
 
     for half in range(2):
         item_arrived(half, 0, 1 - pick)
@@ -123,6 +125,7 @@
             item_arrived(half, du, 1)
             forward(18 + 4 * n + 2 * half, half, du, 0, 1)
             forward(19 + 4 * n + 2 * half, half, du, 0, 3)
+    pl.semaphore_signal(token, inc=1, device_id=(ab, cd ^ 1), device_id_type=MESH)
 
     low_half = lax.rem(iota((8, 256), 1), 16) < 8
 
@@ -142,13 +145,6 @@
         term = term.reshape(OWN * WIR, 2, 8, 256)
         acc[second] += jnp.where(low_half[None], term[:, 0], term[:, 1])
 
-    def tiles(count, dx_of, dz_of):
-        def body(i, carry):
-            tile(dx_of(i), dz_of(i))
-            return carry
-
-        lax.fori_loop(0, count, body, 0)
-
     relays = [(0, 3, 1), (1, 1, 3), (3, 1, 3), (2, 3, 1)]
 
     def relay(n):
@@ -164,17 +160,19 @@
     relay(2)
     for half in range(2):
         pair_arrived(half, 0, 1)
-    tiles(4, lambda i: lax.rem(i // 2 * (2 * i + 1), 4), lambda i: (1 - i // 2) * (2 * i + 1))
+    for dx, dz in ((0, 1), (0, 3), (1, 0), (3, 0)):
+        tile(dx, dz)
     relay(3)
     for half in range(2):
         for du in (1, 3):
             pair_arrived(half, du, 3)
         pair_arrived(half, 2, 1)
-    tiles(4, lambda i: i // 2 * 2 + 1, lambda i: lax.rem(i, 2) * 2 + 1)
+    for dx, dz in ((1, 1), (1, 3), (3, 1), (3, 3)):
+        tile(dx, dz)
 
     diagonal = lax.rem(iota((8, 256), 1), 8) == iota((8, 256), 0)
     spread_pairs = (
-        lax.rem(iota((768, 128), 1), 16) == lax.rem(iota((768, 128), 0), 256) // CB
+        lax.rem(iota((512, 128), 1), 16) == lax.rem(iota((512, 128), 0), 256) // CB
     ).astype(BF16)
     row = iota((72, 128), 0)
     lane = iota((72, 128), 1)
@@ -193,67 +191,46 @@
         16 + frm_slot * 8 + slot_low * 4 + frm_k,
     )
     gather_rows = (to == goal).astype(BF16)
-    gather_rows = jnp.concatenate([gather_rows] * 3, axis=1)
-
-    def msg_copy(peer, block, sender):
+    gather_rows = jnp.concatenate([gather_rows] * 2, axis=1)
+
+    to_copy = cd // 2 * 2 + lax.rem(irrep, 2)
+
+    def sender_tile(of_irrep, of_core, of_slot):
+        return (of_irrep // 2 * 2 + of_core) * GROUP + of_slot
+
+    def msg_copy(peer, block, tile_at):
         return pltpu.make_async_remote_copy(
             src_ref=msgs.at[block],
-            dst_ref=mirror.at[sender],
+            dst_ref=mirror.at[tile_at],
             send_sem=msg_send.at[block],
-            recv_sem=msg_recv.at[sender],
-            device_id=(peer, cd),
-            device_id_type=MESH,
-        )
+            recv_sem=msg_recv.at[tile_at],
+            device_id=(peer, to_copy),
+            device_id_type=MESH,
+        )
+
+    my_tile = sender_tile(irrep, core, slot)
+    stays = to_copy == cd
 
     def finish(dx):
         second = lax.rem(irrep + dx, 4) ^ irrep ^ cd
         folded = jnp.sum(jnp.where(diagonal[None], acc[second], 0.0), axis=1)
-        values = jnp.dot(split3(folded, 1), spread_pairs, preferred_element_type=F32)
+        values = jnp.dot(split2(folded, 1), spread_pairs, preferred_element_type=F32)
         both = jnp.concatenate(
             [jnp.where(own_keep, values, 0.0), jnp.where(msg_keep, values, 0.0)], axis=0
         )
-        placed = jnp.dot(gather_rows, split3(both, 0), preferred_element_type=F32)
-        own[second] = placed[:16].reshape(2, 8, 128)
+        placed = jnp.dot(gather_rows, split2(both, 0), preferred_element_type=F32)
+        tiles = placed[:16].reshape(2, 8, 128)
+        if dx == 2:
+            lates[cd, pl.ds(0, 2)] = tiles
+        else:
+            shares[cd, second] = tiles
         msgs[pl.ds(second * GROUP, GROUP)] = placed[16:].reshape(GROUP, 8, 128)
-
-        def send(i, inner):
+        for i in range(GROUP):
             peer = second * GROUP + i
 
-            @pl.when(peer != ab)
+            @pl.when((peer != ab) | ~stays)
             def _():
-                msg_copy(peer, peer, ab).start()
-
-            return inner
-
-        lax.fori_loop(0, GROUP, send, 0)
-
-    for half in range(2):
-        pair_arrived(half, 0, 2)
-    tile(0, 2)
-    finish(0)
-    for half in range(2):
-        for du in (1, 3):
-            pair_arrived(half, du, 2)
-        pair_arrived(half, 2, 2)
-
-    def rest(i, carry):
-        dx = 2 * i + 1
-        tile(dx, 2)
-        finish(dx)
-        return carry
-
-    lax.fori_loop(0, 2, rest, 0)
-    tiles(4, lambda i: 2, lambda i: i)
-    finish(2)
-    mirror[ab] = msgs[ab]
-
-    def collect(i, carry):
-        msg_copy(ab, ab, ab ^ i).wait_recv()
-        return carry
-
-    lax.fori_loop(1, 32, collect, 0)
-    total = own[...] + jnp.sum(mirror[...].reshape(IRREPS, 2, 4, 8, 128), axis=2)
-    shares[cd] = total
+                msg_copy(peer, peer, my_tile).start()
 
     def share_copy(i, peer, sender):
         return pltpu.make_async_remote_copy(
@@ -265,11 +242,63 @@
             device_id_type=MESH,
         )
 
+    def late_copy(i, peer, sender):
+        return pltpu.make_async_remote_copy(
+            src_ref=lates.at[sender],
+            dst_ref=lates.at[sender],
+            send_sem=late_send.at[i],
+            recv_sem=late_recv.at[sender],
+            device_id=(ab, peer),
+            device_id_type=MESH,
+        )
+
+    pl.semaphore_wait(token, 1)
+    for half in range(2):
+        pair_arrived(half, 0, 2)
+    tile(0, 2)
+    finish(0)
+    for half in range(2):
+        for du in (1, 3):
+            pair_arrived(half, du, 2)
+    for dx, dz in ((1, 2), (3, 2), (2, 0), (2, 1), (2, 3)):
+        tile(dx, dz)
+    for dx in (1, 3):
+        finish(dx)
     for i in range(1, 4):
         share_copy(i, cd ^ i, cd).start()
+    for half in range(2):
+        pair_arrived(half, 2, 2)
+    tile(2, 2)
+    finish(2)
+
+    @pl.when(stays)
+    def _():
+        mirror[my_tile] = msgs[ab]
+
+    def collect(i, carry):
+        @pl.when((i != my_tile) | ~stays)
+        def _():
+            msg_copy(ab, ab, i).wait_recv()
+
+        return carry
+
+    lax.fori_loop(0, 32, collect, 0)
+    lates[cd, pl.ds(2, 4)] = jnp.sum(
+        mirror[...].reshape(2, 2, 2, 4, 8, 128), axis=(1, 3)
+    ).reshape(4, 8, 128)
+    for i in range(1, 4):
+        late_copy(i, cd ^ i, cd).start()
     for i in range(1, 4):
         share_copy(i, cd, cd ^ i).wait_recv()
-    out[...] = (shares[0] + shares[1]) + (shares[2] + shares[3])
+    early = (shares[0] + shares[1]) + (shares[2] + shares[3])
+    for i in range(1, 4):
+        late_copy(i, cd, cd ^ i).wait_recv()
+    for second in range(IRREPS):
+        at = pl.ds(2 + second // 2 * 2, 2)
+        odd = second % 2
+        out[second] = (
+            (early[second] + lates[second ^ 2, pl.ds(0, 2)]) + (lates[odd, at] + lates[odd + 2, at])
+        )
 
     def sent_items(i, carry):
         item_copy(i, 0, ab, ab).wait_send()
@@ -280,14 +309,18 @@
         return carry
 
     def sent_msgs(i, carry):
-        msg_copy(ab, ab ^ i, ab).wait_send()
+        @pl.when((i != ab) | ~stays)
+        def _():
+            msg_copy(ab, i, my_tile).wait_send()
+
         return carry
 
     lax.fori_loop(0, 14, sent_items, 0)
     lax.fori_loop(14, 38, sent_pairs, 0)
-    lax.fori_loop(1, 32, sent_msgs, 0)
+    lax.fori_loop(0, 32, sent_msgs, 0)
     for i in range(1, 4):
         share_copy(i, cd, cd).wait_send()
+        late_copy(i, cd, cd).wait_send()
 
 
 def on_device(integrals, amplitudes, block_sizes):
@@ -306,10 +339,10 @@
             pltpu.VMEM(amplitudes.shape, BF16),
             pltpu.VMEM((2, 32, BLK, NPAIR * CB // 2), BF16),
             pltpu.VMEM((IRREPS, OWN * WIR, 8, 256), F32),
-            pltpu.VMEM((IRREPS, 2, 8, 128), F32),
             pltpu.VMEM((32, 8, 128), F32),
             pltpu.VMEM((32, 8, 128), F32),
             pltpu.VMEM((4, IRREPS, 2, 8, 128), F32),
+            pltpu.VMEM((4, 6, 8, 128), F32),
             pltpu.SemaphoreType.DMA,
             pltpu.SemaphoreType.DMA,
             pltpu.SemaphoreType.DMA((38,)),
@@ -319,6 +352,9 @@
             pltpu.SemaphoreType.DMA((32,)),
             pltpu.SemaphoreType.DMA((4,)),
             pltpu.SemaphoreType.DMA((4,)),
+            pltpu.SemaphoreType.DMA((4,)),
+            pltpu.SemaphoreType.DMA((4,)),
+            pltpu.SemaphoreType.REGULAR,
         ],
         compiler_params=pltpu.CompilerParams(
             collective_id=0, has_side_effects=True, vmem_limit_bytes=56 << 20

time: 45.8 us -> 43.6 us (0.952)
  Pallas kernels: 43.8 us -> 41.7 us
    pallas_call x1, Pallas kernels: 43.8 us -> 41.7 us  [on_device(): pl.pallas_call(kernel, out_shape=jax.ShapeDtypeStruct((IRREPS, 2, 8, 128)...]
where the time goes in v3:
time: 43.6 us; the launch traced here: 43.5 us
  Pallas kernels  41.7 us (96%)
  local copies, waits for them, and re-layouts  1.76 us (4%)
    pallas_call x1, Pallas kernels, on_device(): pl.pallas_call(kernel, out_shape=jax.ShapeDtypeStruct((IRREPS, 2, 8, 128)...  41.7 us
    reshape x1, local copies, waits for them, and re-layouts, on_device(): packed.reshape(IRREPS, 2, 2, 4, 2, 4, NPAIR)[:, :, :, :OWN, :, :OWN]  0.97 us

profile of v3, /device:TPU:1, one launch (start us, length us, event | category | flops | bytes accessed | tf_op | source)
XLA Modules:
  0.0 43.5 jit_solution(9459911740212526033)
XLA Ops:
  0.0 41.7 %ladder.1 = f32[4,2,8,128]{3,2,1,0:T(8,128)} custom-call(s32[4]{0:T(128)} %sizes.1, bf16[16,16,128]{2,1,0:T(8,128)(2,1)} %amps.1, bf16[3,96,128,128]{3,2,1,0:T(8,128)(2,1)} %integrals.1), custom_call_target="tpu_custom_call" | custom-call | tf_op jit(solution)/shard_map/ladder/pallas_call | solution.py:328
  41.7 1.0 %reshape.6 = f32[4,2,2,4,2,4,16]{6,5,4,3,2,1,0:T(4,128)S(1)} reshape(f32[4,2,8,128]{3,2,1,0:T(8,128)} %ladder.1) | data formatting | bytes 65536 | tf_op jit(solution)/shard_map/reshape | solution.py:364
  42.7 0.1 reshape.7
  42.7 0.7 %copy.6 = f32[16,3,96]{2,0,1:T(8,128)} copy(f32[16,3,96]{0,2,1:T(8,128)S(1)} %reshape.7) | data formatting | bytes 36864 | tf_op jit(solution)/shard_map/reshape | solution.py:365
  (1 shorter events, 0.0 us)

commit v4 on v3

--- a/solution.py
+++ b/solution.py
@@ -28,9 +28,9 @@
 
 
 def kernel(
-    sizes, amps, integrals, out, ints, plain, panels, acc, msgs, mirror, shares, lates,
-    ints_sem, plain_sem, send_sem, item_recv, pair_recv, msg_send, msg_recv,
-    share_send, share_recv, late_send, late_recv, token,
+    sizes, amps, integrals, out, ints, plain, panels, acc, given, taken, msgs, mirror, own, halves,
+    ints_sem, plain_sem, send_sem, item_recv, pair_recv, pass_send, pass_recv,
+    msg_send, msg_recv, own_send, own_recv, half_send, half_recv, token,
 ):
     ab = lax.axis_index("ab")
     cd = lax.axis_index("cd")
@@ -41,7 +41,8 @@
     ring = slot // 2
     pick = slot_lane
     core = lax.rem(cd, 2)
-    late = cd ^ 2
+    high = cd // 2
+    other = cd ^ 1
 
     fetch_own = pltpu.make_async_copy(amps, plain, plain_sem)
     fetch_own.start()
@@ -113,7 +114,6 @@
             item_copy(2 * n + half, half, peer_of(half, du, dy), ab).start()
 
     acc[...] = jnp.zeros_like(acc)
-    shares[cd, late] = jnp.zeros((2, 8, 128), F32)
 
     for half in range(2):
         item_arrived(half, 0, 1 - pick)
@@ -125,12 +125,13 @@
             item_arrived(half, du, 1)
             forward(18 + 4 * n + 2 * half, half, du, 0, 1)
             forward(19 + 4 * n + 2 * half, half, du, 0, 3)
-    pl.semaphore_signal(token, inc=1, device_id=(ab, cd ^ 1), device_id_type=MESH)
+    for i in range(1, 4):
+        pl.semaphore_signal(token, inc=1, device_id=(ab, cd ^ i), device_id_type=MESH)
 
     low_half = lax.rem(iota((8, 256), 1), 16) < 8
 
-    def tile(dx, dz):
-        source = lax.rem(irrep + dx, 4)
+    def tile(rel, dz):
+        source = irrep ^ rel
         second = source ^ irrep ^ cd
         at = lax.rem(ring + dz, 4)
         first = source * GROUP + at * 2
@@ -160,15 +161,15 @@
     relay(2)
     for half in range(2):
         pair_arrived(half, 0, 1)
-    for dx, dz in ((0, 1), (0, 3), (1, 0), (3, 0)):
-        tile(dx, dz)
+    for rel, dz in ((0, 1), (0, 3), (1, 0), (3, 0)):
+        tile(rel, dz)
     relay(3)
     for half in range(2):
         for du in (1, 3):
             pair_arrived(half, du, 3)
         pair_arrived(half, 2, 1)
-    for dx, dz in ((1, 1), (1, 3), (3, 1), (3, 3)):
-        tile(dx, dz)
+    for rel, dz in ((1, 1), (1, 3), (3, 1), (3, 3)):
+        tile(rel, dz)
 
     diagonal = lax.rem(iota((8, 256), 1), 8) == iota((8, 256), 0)
     spread_pairs = (
@@ -193,79 +194,87 @@
     gather_rows = (to == goal).astype(BF16)
     gather_rows = jnp.concatenate([gather_rows] * 2, axis=1)
 
-    to_copy = cd // 2 * 2 + lax.rem(irrep, 2)
-
-    def sender_tile(of_irrep, of_core, of_slot):
-        return (of_irrep // 2 * 2 + of_core) * GROUP + of_slot
-
-    def msg_copy(peer, block, tile_at):
+    to_core = lax.rem(irrep, 2)
+
+    def pass_copy(n, peer):
+        return pltpu.make_async_remote_copy(
+            src_ref=given.at[n],
+            dst_ref=taken.at[n],
+            send_sem=pass_send.at[n],
+            recv_sem=pass_recv.at[n],
+            device_id=(ab, peer),
+            device_id_type=MESH,
+        )
+
+    def msg_copy(block, to_high, tile_at):
         return pltpu.make_async_remote_copy(
             src_ref=msgs.at[block],
             dst_ref=mirror.at[tile_at],
-            send_sem=msg_send.at[block],
+            send_sem=msg_send.at[to_high, block],
             recv_sem=msg_recv.at[tile_at],
-            device_id=(peer, to_copy),
-            device_id_type=MESH,
-        )
-
-    my_tile = sender_tile(irrep, core, slot)
-    stays = to_copy == cd
-
-    def finish(dx):
-        second = lax.rem(irrep + dx, 4) ^ irrep ^ cd
+            device_id=(block, to_high * 2 + to_core),
+            device_id_type=MESH,
+        )
+
+    my_tile = (irrep // 2 * 2 + high) * GROUP + slot
+    stays = to_core == core
+
+    def own_copy(n, peer, sender):
+        return pltpu.make_async_remote_copy(
+            src_ref=own.at[sender, n],
+            dst_ref=own.at[sender, n],
+            send_sem=own_send.at[n],
+            recv_sem=own_recv.at[n],
+            device_id=(ab, peer),
+            device_id_type=MESH,
+        )
+
+    def half_copy(peer, sender):
+        return pltpu.make_async_remote_copy(
+            src_ref=halves.at[sender],
+            dst_ref=halves.at[sender],
+            send_sem=half_send,
+            recv_sem=half_recv,
+            device_id=(ab, peer),
+            device_id_type=MESH,
+        )
+
+    def finish(rel):
+        second = rel ^ cd
         folded = jnp.sum(jnp.where(diagonal[None], acc[second], 0.0), axis=1)
         values = jnp.dot(split2(folded, 1), spread_pairs, preferred_element_type=F32)
         both = jnp.concatenate(
             [jnp.where(own_keep, values, 0.0), jnp.where(msg_keep, values, 0.0)], axis=0
         )
         placed = jnp.dot(gather_rows, split2(both, 0), preferred_element_type=F32)
-        tiles = placed[:16].reshape(2, 8, 128)
-        if dx == 2:
-            lates[cd, pl.ds(0, 2)] = tiles
-        else:
-            shares[cd, second] = tiles
+        if rel % 2:
+            given[rel // 2] = placed
+            pass_copy(rel // 2, other).start()
+            return
+        pass_copy(rel // 2, other).wait_recv()
+        placed = placed + taken[rel // 2]
         msgs[pl.ds(second * GROUP, GROUP)] = placed[16:].reshape(GROUP, 8, 128)
         for i in range(GROUP):
-            peer = second * GROUP + i
-
-            @pl.when((peer != ab) | ~stays)
-            def _():
-                msg_copy(peer, peer, my_tile).start()
-
-    def share_copy(i, peer, sender):
-        return pltpu.make_async_remote_copy(
-            src_ref=shares.at[sender],
-            dst_ref=shares.at[sender],
-            send_sem=share_send.at[i],
-            recv_sem=share_recv.at[sender],
-            device_id=(ab, peer),
-            device_id_type=MESH,
-        )
-
-    def late_copy(i, peer, sender):
-        return pltpu.make_async_remote_copy(
-            src_ref=lates.at[sender],
-            dst_ref=lates.at[sender],
-            send_sem=late_send.at[i],
-            recv_sem=late_recv.at[sender],
-            device_id=(ab, peer),
-            device_id_type=MESH,
-        )
-
-    pl.semaphore_wait(token, 1)
-    for half in range(2):
-        pair_arrived(half, 0, 2)
-    tile(0, 2)
+            block = second * GROUP + i
+            for to_high in range(2):
+
+                @pl.when((block != ab) | (to_high * 2 + to_core != cd))
+                def _():
+                    msg_copy(block, to_high, my_tile).start()
+
+        at = second // 2
+        own[high, at] = placed[:16].reshape(2, 8, 128)
+        own_copy(at, cd ^ 2, high).start()
+
+    for half in range(2):
+        for du in (0, 1, 3):
+            pair_arrived(half, du, 2)
+    for rel, dz in ((1, 2), (3, 2), (0, 2), (2, 0), (2, 1), (2, 3)):
+        tile(rel, dz)
+    finish(1)
+    finish(3)
+    pl.semaphore_wait(token, 3)
     finish(0)
-    for half in range(2):
-        for du in (1, 3):
-            pair_arrived(half, du, 2)
-    for dx, dz in ((1, 2), (3, 2), (2, 0), (2, 1), (2, 3)):
-        tile(dx, dz)
-    for dx in (1, 3):
-        finish(dx)
-    for i in range(1, 4):
-        share_copy(i, cd ^ i, cd).start()
     for half in range(2):
         pair_arrived(half, 2, 2)
     tile(2, 2)
@@ -278,27 +287,19 @@
     def collect(i, carry):
         @pl.when((i != my_tile) | ~stays)
         def _():
-            msg_copy(ab, ab, i).wait_recv()
+            msg_copy(ab, 0, i).wait_recv()
 
         return carry
 
     lax.fori_loop(0, 32, collect, 0)
-    lates[cd, pl.ds(2, 4)] = jnp.sum(
-        mirror[...].reshape(2, 2, 2, 4, 8, 128), axis=(1, 3)
-    ).reshape(4, 8, 128)
-    for i in range(1, 4):
-        late_copy(i, cd ^ i, cd).start()
-    for i in range(1, 4):
-        share_copy(i, cd, cd ^ i).wait_recv()
-    early = (shares[0] + shares[1]) + (shares[2] + shares[3])
-    for i in range(1, 4):
-        late_copy(i, cd, cd ^ i).wait_recv()
+    mirrored = jnp.sum(mirror[...].reshape(2, 2, 2, 4, 8, 128), axis=(1, 3))
+    for n in range(2):
+        own_copy(n, cd, 1 - high).wait_recv()
+    halves[core] = (own[0] + own[1]) + mirrored
+    half_copy(other, core).start()
+    half_copy(cd, 1 - core).wait_recv()
     for second in range(IRREPS):
-        at = pl.ds(2 + second // 2 * 2, 2)
-        odd = second % 2
-        out[second] = (
-            (early[second] + lates[second ^ 2, pl.ds(0, 2)]) + (lates[odd, at] + lates[odd + 2, at])
-        )
+        out[second] = halves[second % 2, second // 2]
 
     def sent_items(i, carry):
         item_copy(i, 0, ab, ab).wait_send()
@@ -309,18 +310,23 @@
         return carry
 
     def sent_msgs(i, carry):
-        @pl.when((i != ab) | ~stays)
-        def _():
-            msg_copy(ab, i, my_tile).wait_send()
+        for to_high in range(2):
+            for n in range(2):
+                block = (core + 2 * n) * GROUP + i
+
+                @pl.when((block != ab) | (to_high * 2 + to_core != cd))
+                def _():
+                    msg_copy(block, to_high, my_tile).wait_send()
 
         return carry
 
     lax.fori_loop(0, 14, sent_items, 0)
     lax.fori_loop(14, 38, sent_pairs, 0)
-    lax.fori_loop(0, 32, sent_msgs, 0)
-    for i in range(1, 4):
-        share_copy(i, cd, cd).wait_send()
-        late_copy(i, cd, cd).wait_send()
+    lax.fori_loop(0, GROUP, sent_msgs, 0)
+    for n in range(2):
+        pass_copy(n, cd).wait_send()
+        own_copy(n, cd, high).wait_send()
+    half_copy(cd, core).wait_send()
 
 
 def on_device(integrals, amplitudes, block_sizes):
@@ -339,21 +345,25 @@
             pltpu.VMEM(amplitudes.shape, BF16),
             pltpu.VMEM((2, 32, BLK, NPAIR * CB // 2), BF16),
             pltpu.VMEM((IRREPS, OWN * WIR, 8, 256), F32),
+            pltpu.VMEM((2, 80, 128), F32),
+            pltpu.VMEM((2, 80, 128), F32),
             pltpu.VMEM((32, 8, 128), F32),
             pltpu.VMEM((32, 8, 128), F32),
-            pltpu.VMEM((4, IRREPS, 2, 8, 128), F32),
-            pltpu.VMEM((4, 6, 8, 128), F32),
+            pltpu.VMEM((2, 2, 2, 8, 128), F32),
+            pltpu.VMEM((2, 2, 2, 8, 128), F32),
             pltpu.SemaphoreType.DMA,
             pltpu.SemaphoreType.DMA,
             pltpu.SemaphoreType.DMA((38,)),
             pltpu.SemaphoreType.DMA((2, 32)),
             pltpu.SemaphoreType.DMA((2, 16)),
+            pltpu.SemaphoreType.DMA((2,)),
+            pltpu.SemaphoreType.DMA((2,)),
+            pltpu.SemaphoreType.DMA((2, 32)),
             pltpu.SemaphoreType.DMA((32,)),
-            pltpu.SemaphoreType.DMA((32,)),
-            pltpu.SemaphoreType.DMA((4,)),
-            pltpu.SemaphoreType.DMA((4,)),
-            pltpu.SemaphoreType.DMA((4,)),
-            pltpu.SemaphoreType.DMA((4,)),
+            pltpu.SemaphoreType.DMA((2,)),
+            pltpu.SemaphoreType.DMA((2,)),
+            pltpu.SemaphoreType.DMA,
+            pltpu.SemaphoreType.DMA,
             pltpu.SemaphoreType.REGULAR,
         ],
         compiler_params=pltpu.CompilerParams(

time: 43.6 us -> 42.1 us (0.966)
  Pallas kernels: 41.7 us -> 40.1 us
    pallas_call x1, Pallas kernels: 41.7 us -> 40.1 us  [on_device(): pl.pallas_call(kernel, out_shape=jax.ShapeDtypeStruct((IRREPS, 2, 8, 128)...]
where the time goes in v4:
time: 42.1 us; the launch traced here: 41.9 us
  Pallas kernels  40.1 us (95%)
  local copies, waits for them, and re-layouts  1.76 us (4%)
    pallas_call x1, Pallas kernels, on_device(): pl.pallas_call(kernel, out_shape=jax.ShapeDtypeStruct((IRREPS, 2, 8, 128)...  40.1 us
    reshape x1, local copies, waits for them, and re-layouts, on_device(): packed.reshape(IRREPS, 2, 2, 4, 2, 4, NPAIR)[:, :, :, :OWN, :, :OWN]  0.97 us

profile of v4, /device:TPU:1, one launch (start us, length us, event | category | flops | bytes accessed | tf_op | source)
XLA Modules:
  0.0 41.9 jit_solution(15713514338441981007)
XLA Ops:
  0.0 40.1 %ladder.1 = f32[4,2,8,128]{3,2,1,0:T(8,128)} custom-call(s32[4]{0:T(128)} %sizes.1, bf16[16,16,128]{2,1,0:T(8,128)(2,1)} %amps.1, bf16[3,96,128,128]{3,2,1,0:T(8,128)(2,1)} %integrals.1), custom_call_target="tpu_custom_call" | custom-call | tf_op jit(solution)/shard_map/ladder/pallas_call | solution.py:334
  40.2 1.0 %reshape.6 = f32[4,2,2,4,2,4,16]{6,5,4,3,2,1,0:T(4,128)S(1)} reshape(f32[4,2,8,128]{3,2,1,0:T(8,128)} %ladder.1) | data formatting | bytes 65536 | tf_op jit(solution)/shard_map/reshape | solution.py:374
  41.2 0.1 reshape.7
  41.2 0.7 %copy.6 = f32[16,3,96]{2,0,1:T(8,128)} copy(f32[16,3,96]{0,2,1:T(8,128)S(1)} %reshape.7) | data formatting | bytes 36864 | tf_op jit(solution)/shard_map/reshape | solution.py:375
  (1 shorter events, 0.0 us)

commit v5 on v4

--- a/solution.py
+++ b/solution.py
@@ -29,7 +29,7 @@
 
 def kernel(
     sizes, amps, integrals, out, ints, plain, panels, acc, given, taken, msgs, mirror, own, halves,
-    ints_sem, plain_sem, send_sem, item_recv, pair_recv, pass_send, pass_recv,
+    ints_sem, plain_sem, send_sem, item_recv, pass_send, pass_recv,
     msg_send, msg_recv, own_send, own_recv, half_send, half_recv, token,
 ):
     ab = lax.axis_index("ab")
@@ -47,22 +47,20 @@
     fetch_own = pltpu.make_async_copy(amps, plain, plain_sem)
     fetch_own.start()
 
-    def place(half, du, dv, y):
+    along_x = [lax.rem(irrep + d, 4) * GROUP for d in range(4)]
+    along_z = [lax.rem(ring + d, 4) * 2 for d in range(4)]
+    along_y = [pick, 1 - pick]
+
+    def place(half, du, dv, dy):
         if half == 0:
-            return lax.rem(irrep + dv, 4) * GROUP + lax.rem(ring + du, 4) * 2 + y
-        return lax.rem(irrep + du, 4) * GROUP + lax.rem(ring + dv, 4) * 2 + y
-
-    plane = [(0, 1), (1, 0), (3, 0), (1, 1), (3, 1), (2, 0), (2, 1)]
-
-    def peer_of(half, du, dy):
-        return place(half, du, 0, lax.rem(pick + dy, 2))
+            return along_x[dv] + along_z[du] + along_y[dy]
+        return along_x[du] + along_z[dv] + along_y[dy]
 
     barrier = pltpu.get_barrier_semaphore()
-    for half in range(2):
-        for du, dy in plane[half:]:
-            pl.semaphore_signal(
-                barrier, inc=1, device_id=(peer_of(half, du, dy), cd), device_id_type=MESH
-            )
+    for du, dv, dy in ((1, 0, 0), (3, 0, 0), (2, 0, 0), (0, 1, 0), (0, 3, 0), (0, 2, 0), (0, 0, 1)):
+        pl.semaphore_signal(
+            barrier, inc=1, device_id=(place(0, du, dv, dy), cd), device_id_type=MESH
+        )
     for i in range(1, 4):
         pl.semaphore_signal(barrier, inc=1, device_id=(ab, cd ^ i), device_id_type=MESH)
 
@@ -88,45 +86,71 @@
             device_id_type=MESH,
         )
 
-    def pair_copy(i, half, peer, first):
-        return pltpu.make_async_remote_copy(
-            src_ref=panels.at[half, pl.ds(first, 2)],
-            dst_ref=panels.at[half, pl.ds(first, 2)],
-            send_sem=send_sem.at[i],
-            recv_sem=pair_recv.at[half, first // 2],
-            device_id=(peer, cd),
-            device_id_type=MESH,
-        )
-
-    def item_arrived(half, du, y):
-        item_copy(0, half, ab, place(half, du, 0, y)).wait_recv()
-
-    def pair_arrived(half, du, dv):
-        pair_copy(0, half, ab, place(half, du, dv, 0)).wait_recv()
-
-    def forward(i, half, du, dv, to):
-        pair_copy(i, half, place(half, 0, to, pick), place(half, du, dv, 0)).start()
-
-    pl.semaphore_wait(barrier, 16)
-
-    for n, (du, dy) in enumerate(plane):
-        for half in range(2):
-            item_copy(2 * n + half, half, peer_of(half, du, dy), ab).start()
+    sent = []
+
+    def send(half, block, to):
+        item_copy(len(sent), half, place(half, *to), place(half, *block)).start()
+        sent.append(half)
+
+    def arrived(half, *block):
+        item_copy(0, half, ab, place(half, *block)).wait_recv()
+
+    def onward(half, du, dy):
+        send(half, (du, 0, dy), (0, 1, 0))
+        send(half, (du, 0, dy), (0, 3, 0))
+        if (du, dy) == (2, 1):
+            send(half, (du, 0, dy), (0, 2, 0))
+
+    def first_ring(du):
+        for half in range(2):
+            arrived(half, du, 0, 0)
+            send(half, (du, 0, 0), (0, 0, 1))
+            onward(half, du, 0)
+
+    def from_partner(du):
+        for half in range(2):
+            arrived(half, du, 0, 1)
+            onward(half, du, 1)
+
+    from_below = ((0, 0), (2, 0), (1, 1), (3, 1))
+
+    def relay(du, dy):
+        dv = 3 if (du, dy) in from_below else 1
+        for half in range(2):
+            arrived(half, du, dv, dy)
+            send(half, (du, dv, dy), (0, 4 - dv, 0))
+
+    def rest_arrived(du, dy):
+        dv = 1 if (du, dy) in from_below else 3
+        for half in range(2):
+            arrived(half, du, dv, dy)
+
+    def far_arrived(du):
+        for half in range(2):
+            for dy in range(2):
+                arrived(half, du, 2, dy)
+
+    pl.semaphore_wait(barrier, 10)
+
+    for du in (1, 3):
+        for half in range(2):
+            send(half, (0, 0, 0), (du, 0, 0))
+    for half in range(2):
+        onward(half, 0, 0)
+    for half in range(2):
+        send(half, (0, 0, 0), (0, 0, 1))
+    for half in range(2):
+        send(half, (0, 0, 0), (2, 0, 0))
 
     acc[...] = jnp.zeros_like(acc)
 
-    for half in range(2):
-        item_arrived(half, 0, 1 - pick)
-        forward(14 + 2 * half, half, 0, 0, 1)
-        forward(15 + 2 * half, half, 0, 0, 3)
-    for n, du in enumerate((1, 3, 2)):
-        for half in range(2):
-            item_arrived(half, du, 0)
-            item_arrived(half, du, 1)
-            forward(18 + 4 * n + 2 * half, half, du, 0, 1)
-            forward(19 + 4 * n + 2 * half, half, du, 0, 3)
-    for i in range(1, 4):
-        pl.semaphore_signal(token, inc=1, device_id=(ab, cd ^ i), device_id_type=MESH)
+    first_ring(1)
+    first_ring(3)
+    from_partner(0)
+    relay(0, 0)
+    first_ring(2)
+    from_partner(1)
+    from_partner(3)
 
     low_half = lax.rem(iota((8, 256), 1), 16) < 8
 
@@ -146,30 +170,30 @@
         term = term.reshape(OWN * WIR, 2, 8, 256)
         acc[second] += jnp.where(low_half[None], term[:, 0], term[:, 1])
 
-    relays = [(0, 3, 1), (1, 1, 3), (3, 1, 3), (2, 3, 1)]
-
-    def relay(n):
-        du, dv, to = relays[n]
-        for half in range(2):
-            pair_arrived(half, du, dv)
-            forward(30 + 2 * n + half, half, du, dv, to)
-
-    relay(0)
     fetch.wait()
     tile(0, 0)
-    relay(1)
-    relay(2)
-    for half in range(2):
-        pair_arrived(half, 0, 1)
+    relay(1, 0)
+    relay(3, 0)
+    relay(0, 1)
+    from_partner(2)
+    for i in range(1, 4):
+        pl.semaphore_signal(token, inc=1, device_id=(ab, cd ^ i), device_id_type=MESH)
+    rest_arrived(0, 0)
+    rest_arrived(0, 1)
     for rel, dz in ((0, 1), (0, 3), (1, 0), (3, 0)):
         tile(rel, dz)
-    relay(3)
-    for half in range(2):
-        for du in (1, 3):
-            pair_arrived(half, du, 3)
-        pair_arrived(half, 2, 1)
+    relay(2, 0)
+    relay(1, 1)
+    relay(3, 1)
+    for du in (1, 3):
+        for dy in range(2):
+            rest_arrived(du, dy)
     for rel, dz in ((1, 1), (1, 3), (3, 1), (3, 3)):
         tile(rel, dz)
+    rest_arrived(2, 0)
+    for half in range(2):
+        for dv in (1, 3):
+            arrived(half, 2, dv, 1)
 
     diagonal = lax.rem(iota((8, 256), 1), 8) == iota((8, 256), 0)
     spread_pairs = (
@@ -266,17 +290,15 @@
         own[high, at] = placed[:16].reshape(2, 8, 128)
         own_copy(at, cd ^ 2, high).start()
 
-    for half in range(2):
-        for du in (0, 1, 3):
-            pair_arrived(half, du, 2)
+    for du in (0, 1, 3):
+        far_arrived(du)
     for rel, dz in ((1, 2), (3, 2), (0, 2), (2, 0), (2, 1), (2, 3)):
         tile(rel, dz)
     finish(1)
     finish(3)
     pl.semaphore_wait(token, 3)
     finish(0)
-    for half in range(2):
-        pair_arrived(half, 2, 2)
+    far_arrived(2)
     tile(2, 2)
     finish(2)
 
@@ -305,10 +327,6 @@
         item_copy(i, 0, ab, ab).wait_send()
         return carry
 
-    def sent_pairs(i, carry):
-        pair_copy(i, 0, ab, 0).wait_send()
-        return carry
-
     def sent_msgs(i, carry):
         for to_high in range(2):
             for n in range(2):
@@ -320,8 +338,7 @@
 
         return carry
 
-    lax.fori_loop(0, 14, sent_items, 0)
-    lax.fori_loop(14, 38, sent_pairs, 0)
+    lax.fori_loop(0, len(sent), sent_items, 0)
     lax.fori_loop(0, GROUP, sent_msgs, 0)
     for n in range(2):
         pass_copy(n, cd).wait_send()
@@ -353,9 +370,8 @@
             pltpu.VMEM((2, 2, 2, 8, 128), F32),
             pltpu.SemaphoreType.DMA,
             pltpu.SemaphoreType.DMA,
-            pltpu.SemaphoreType.DMA((38,)),
+            pltpu.SemaphoreType.DMA((62,)),
             pltpu.SemaphoreType.DMA((2, 32)),
-            pltpu.SemaphoreType.DMA((2, 16)),
             pltpu.SemaphoreType.DMA((2,)),
             pltpu.SemaphoreType.DMA((2,)),
             pltpu.SemaphoreType.DMA((2, 32)),

time: 42.1 us -> 38.8 us (0.922)
  Pallas kernels: 40.1 us -> 36.9 us
    pallas_call x1, Pallas kernels: 40.1 us -> 36.9 us  [on_device(): pl.pallas_call(kernel, out_shape=jax.ShapeDtypeStruct((IRREPS, 2, 8, 128)...]
where the time goes in v5:
time: 38.8 us; the launch traced here: 38.7 us
  Pallas kernels  36.9 us (95%)
  local copies, waits for them, and re-layouts  1.76 us (5%)
    pallas_call x1, Pallas kernels, on_device(): pl.pallas_call(kernel, out_shape=jax.ShapeDtypeStruct((IRREPS, 2, 8, 128)...  36.9 us
    reshape x1, local copies, waits for them, and re-layouts, on_device(): packed.reshape(IRREPS, 2, 2, 4, 2, 4, NPAIR)[:, :, :, :OWN, :, :OWN]  0.97 us

profile of v5, /device:TPU:1, one launch (start us, length us, event | category | flops | bytes accessed | tf_op | source)
XLA Modules:
  0.0 38.7 jit_solution(16443961245885999715)
XLA Ops:
  0.0 36.9 %ladder.1 = f32[4,2,8,128]{3,2,1,0:T(8,128)} custom-call(s32[4]{0:T(128)} %sizes.1, bf16[16,16,128]{2,1,0:T(8,128)(2,1)} %amps.1, bf16[3,96,128,128]{3,2,1,0:T(8,128)(2,1)} %integrals.1), custom_call_target="tpu_custom_call" | custom-call | tf_op jit(solution)/shard_map/ladder/pallas_call | solution.py:351
  36.9 1.0 %reshape.6 = f32[4,2,2,4,2,4,16]{6,5,4,3,2,1,0:T(4,128)S(1)} reshape(f32[4,2,8,128]{3,2,1,0:T(8,128)} %ladder.1) | data formatting | bytes 65536 | tf_op jit(solution)/shard_map/reshape | solution.py:390
  37.9 0.1 reshape.7
  37.9 0.7 %copy.6 = f32[16,3,96]{2,0,1:T(8,128)} copy(f32[16,3,96]{0,2,1:T(8,128)S(1)} %reshape.7) | data formatting | bytes 36864 | tf_op jit(solution)/shard_map/reshape | solution.py:391
  (1 shorter events, 0.0 us)

commit v6 on v5

--- a/solution.py
+++ b/solution.py
@@ -29,6 +29,7 @@
 
 def kernel(
     sizes, amps, integrals, out, ints, plain, panels, acc, given, taken, msgs, mirror, own, halves,
+    spread_pairs, keep_rows, gather_rows,
     ints_sem, plain_sem, send_sem, item_recv, pass_send, pass_recv,
     msg_send, msg_recv, own_send, own_recv, half_send, half_recv, token,
 ):
@@ -70,7 +71,7 @@
     row_limit = sizes[irrep] - slot * CB
     col_limit = sizes[cd]
     shape = (NPAIR * CB, BLK)
-    keep = (lax.rem(iota(shape, 0), CB) < row_limit) & (iota(shape, 1) < col_limit)
+    keep = ((iota(shape, 0) & (CB - 1)) < row_limit) & (iota(shape, 1) < col_limit)
     fetch_own.wait()
     turned = jnp.where(keep, plain[...].reshape(shape).astype(F32), 0.0).T.astype(BF16)
     panels[0, ab] = turned[:, :128]
@@ -101,34 +102,35 @@
         if (du, dy) == (2, 1):
             send(half, (du, 0, dy), (0, 2, 0))
 
-    def first_ring(du):
-        for half in range(2):
+    both = (0, 1)
+
+    def first_ring(du, halves=both):
+        for half in halves:
             arrived(half, du, 0, 0)
             send(half, (du, 0, 0), (0, 0, 1))
             onward(half, du, 0)
 
-    def from_partner(du):
-        for half in range(2):
+    def from_partner(du, halves=both):
+        for half in halves:
             arrived(half, du, 0, 1)
             onward(half, du, 1)
 
     from_below = ((0, 0), (2, 0), (1, 1), (3, 1))
 
-    def relay(du, dy):
+    def relay(du, dy, halves=both):
         dv = 3 if (du, dy) in from_below else 1
-        for half in range(2):
+        for half in halves:
             arrived(half, du, dv, dy)
             send(half, (du, dv, dy), (0, 4 - dv, 0))
 
-    def rest_arrived(du, dy):
+    def rest_arrived(du, dy, halves=both):
         dv = 1 if (du, dy) in from_below else 3
-        for half in range(2):
+        for half in halves:
             arrived(half, du, dv, dy)
 
-    def far_arrived(du):
-        for half in range(2):
-            for dy in range(2):
-                arrived(half, du, 2, dy)
+    def far_arrived(half, du):
+        for dy in range(2):
+            arrived(half, du, 2, dy)
 
     pl.semaphore_wait(barrier, 10)
 
@@ -143,16 +145,37 @@
         send(half, (0, 0, 0), (2, 0, 0))
 
     acc[...] = jnp.zeros_like(acc)
+    spread_pairs[...] = (
+        (iota((512, 128), 1) & 15) == ((iota((512, 128), 0) & 255) >> 4)
+    ).astype(BF16)
+    lane = iota((72, 128), 1)
+    lane_slot, lane_item = lane >> 6, (lane >> 4) & 3
+    row_a, row_b = iota((72, 128), 0) // WIR, lax.rem(iota((72, 128), 0), WIR)
+    own_row = (lane_slot == ((row_b // OWN) & 1)) & (lane_item == lax.rem(row_b, OWN))
+    keep_rows[pl.ds(0, 72)] = own_row.astype(F32)
+    keep_rows[pl.ds(72, 72)] = ((lane_slot == slot_lane) & (lane_item == row_a)).astype(F32)
+    frm = iota((80, 144), 1)
+    frm_row = lax.rem(frm, 72)
+    frm_a, frm_b = frm_row // WIR, lax.rem(frm_row, WIR)
+    frm_slot, frm_k = frm_b // OWN, lax.rem(frm_b, OWN)
+    goal = jnp.where(
+        frm < 72,
+        (frm_slot >> 2) * 8 + ((frm_slot >> 1) & 1) * 4 + frm_a,
+        16 + frm_slot * 8 + slot_low * 4 + frm_k,
+    )
+    goal = (iota((80, 144), 0) == goal).astype(BF16)
+    gather_rows[...] = jnp.concatenate([goal, goal], axis=1)
+    diagonal = (iota((8, 256), 1) & 7) == iota((8, 256), 0)
+    low_half = (iota((8, 256), 1) & 15) < 8
 
     first_ring(1)
     first_ring(3)
     from_partner(0)
     relay(0, 0)
-    first_ring(2)
+    first_ring(2, (0,))
     from_partner(1)
     from_partner(3)
-
-    low_half = lax.rem(iota((8, 256), 1), 16) < 8
+    from_partner(2, (0,))
 
     def tile(rel, dz):
         source = irrep ^ rel
@@ -175,14 +198,15 @@
     relay(1, 0)
     relay(3, 0)
     relay(0, 1)
-    from_partner(2)
+    first_ring(2, (1,))
+    from_partner(2, (1,))
     for i in range(1, 4):
         pl.semaphore_signal(token, inc=1, device_id=(ab, cd ^ i), device_id_type=MESH)
     rest_arrived(0, 0)
     rest_arrived(0, 1)
     for rel, dz in ((0, 1), (0, 3), (1, 0), (3, 0)):
         tile(rel, dz)
-    relay(2, 0)
+    relay(2, 0, (0,))
     relay(1, 1)
     relay(3, 1)
     for du in (1, 3):
@@ -190,33 +214,7 @@
             rest_arrived(du, dy)
     for rel, dz in ((1, 1), (1, 3), (3, 1), (3, 3)):
         tile(rel, dz)
-    rest_arrived(2, 0)
-    for half in range(2):
-        for dv in (1, 3):
-            arrived(half, 2, dv, 1)
-
-    diagonal = lax.rem(iota((8, 256), 1), 8) == iota((8, 256), 0)
-    spread_pairs = (
-        lax.rem(iota((512, 128), 1), 16) == lax.rem(iota((512, 128), 0), 256) // CB
-    ).astype(BF16)
-    row = iota((72, 128), 0)
-    lane = iota((72, 128), 1)
-    lane_slot, lane_item = lane // 64, lax.rem(lane, 64) // 16
-    row_a, row_b = row // WIR, lax.rem(row, WIR)
-    own_keep = (lane_slot == lax.rem(row_b // OWN, 2)) & (lane_item == lax.rem(row_b, OWN))
-    msg_keep = (lane_slot == slot_lane) & (lane_item == row_a)
-    to = iota((80, 144), 0)
-    frm = iota((80, 144), 1)
-    frm_row = lax.rem(frm, 72)
-    frm_a, frm_b = frm_row // WIR, lax.rem(frm_row, WIR)
-    frm_slot, frm_k = frm_b // OWN, lax.rem(frm_b, OWN)
-    goal = jnp.where(
-        frm < 72,
-        (frm_slot // 4) * 8 + lax.rem(frm_slot // 2, 2) * 4 + frm_a,
-        16 + frm_slot * 8 + slot_low * 4 + frm_k,
-    )
-    gather_rows = (to == goal).astype(BF16)
-    gather_rows = jnp.concatenate([gather_rows] * 2, axis=1)
+    relay(2, 0, (1,))
 
     to_core = lax.rem(irrep, 2)
 
@@ -263,18 +261,26 @@
             device_id_type=MESH,
         )
 
+    def ending(*rels):
+        folded = [
+            jnp.sum(jnp.where(diagonal[None], acc[rel ^ cd], 0.0), axis=1) for rel in rels
+        ]
+        values = jnp.dot(
+            split2(jnp.concatenate(folded, axis=0), 1),
+            spread_pairs[...],
+            preferred_element_type=F32,
+        )
+        kept = []
+        for n in range(len(rels)):
+            part = values[n * 72 : (n + 1) * 72]
+            kept.append(jnp.concatenate([part, part], axis=0) * keep_rows[...])
+        return jnp.dot(
+            gather_rows[...], split2(jnp.concatenate(kept, axis=1), 0), preferred_element_type=F32
+        )
+
     def finish(rel):
         second = rel ^ cd
-        folded = jnp.sum(jnp.where(diagonal[None], acc[second], 0.0), axis=1)
-        values = jnp.dot(split2(folded, 1), spread_pairs, preferred_element_type=F32)
-        both = jnp.concatenate(
-            [jnp.where(own_keep, values, 0.0), jnp.where(msg_keep, values, 0.0)], axis=0
-        )
-        placed = jnp.dot(gather_rows, split2(both, 0), preferred_element_type=F32)
-        if rel % 2:
-            given[rel // 2] = placed
-            pass_copy(rel // 2, other).start()
-            return
+        placed = ending(rel)
         pass_copy(rel // 2, other).wait_recv()
         placed = placed + taken[rel // 2]
         msgs[pl.ds(second * GROUP, GROUP)] = placed[16:].reshape(GROUP, 8, 128)
@@ -290,15 +296,29 @@
         own[high, at] = placed[:16].reshape(2, 8, 128)
         own_copy(at, cd ^ 2, high).start()
 
-    for du in (0, 1, 3):
-        far_arrived(du)
-    for rel, dz in ((1, 2), (3, 2), (0, 2), (2, 0), (2, 1), (2, 3)):
+    far_arrived(1, 0)
+    rest_arrived(2, 0, (0,))
+    for dv in (1, 3):
+        arrived(0, 2, dv, 1)
+    far_arrived(1, 1)
+    far_arrived(1, 3)
+    for rel, dz in ((1, 2), (3, 2), (0, 2)):
         tile(rel, dz)
-    finish(1)
-    finish(3)
+    passed = ending(1, 3)
+    for n in range(2):
+        given[n] = passed[:, n * 128 : (n + 1) * 128]
+        pass_copy(n, other).start()
     pl.semaphore_wait(token, 3)
     finish(0)
-    far_arrived(2)
+    rest_arrived(2, 0, (1,))
+    for dv in (1, 3):
+        arrived(1, 2, dv, 1)
+    for du in (0, 1, 3):
+        far_arrived(0, du)
+    for dz in (0, 1, 3):
+        tile(2, dz)
+    far_arrived(0, 2)
+    far_arrived(1, 2)
     tile(2, 2)
     finish(2)
 
@@ -368,6 +388,9 @@
             pltpu.VMEM((32, 8, 128), F32),
             pltpu.VMEM((2, 2, 2, 8, 128), F32),
             pltpu.VMEM((2, 2, 2, 8, 128), F32),
+            pltpu.VMEM((512, 128), BF16),
+            pltpu.VMEM((144, 128), F32),
+            pltpu.VMEM((80, 288), BF16),
             pltpu.SemaphoreType.DMA,
             pltpu.SemaphoreType.DMA,
             pltpu.SemaphoreType.DMA((62,)),

time: 38.8 us -> 39.7 us (1.023)
  Pallas kernels: 36.9 us -> 37.7 us
    pallas_call x1, Pallas kernels: 36.9 us -> 37.7 us  [on_device(): pl.pallas_call(kernel, out_shape=jax.ShapeDtypeStruct((IRREPS, 2, 8, 128)...]
where the time goes in v6:
time: 39.7 us; the launch traced here: 39.5 us
  Pallas kernels  37.7 us (95%)
  local copies, waits for them, and re-layouts  1.76 us (4%)
    pallas_call x1, Pallas kernels, on_device(): pl.pallas_call(kernel, out_shape=jax.ShapeDtypeStruct((IRREPS, 2, 8, 128)...  37.7 us
    reshape x1, local copies, waits for them, and re-layouts, on_device(): packed.reshape(IRREPS, 2, 2, 4, 2, 4, NPAIR)[:, :, :, :OWN, :, :OWN]  0.97 us

profile of v6, /device:TPU:1, one launch (start us, length us, event | category | flops | bytes accessed | tf_op | source)
XLA Modules:
  0.0 39.5 jit_solution(3914067732476145685)
XLA Ops:
  0.0 37.7 %ladder.1 = f32[4,2,8,128]{3,2,1,0:T(8,128)} custom-call(s32[4]{0:T(128)} %sizes.1, bf16[16,16,128]{2,1,0:T(8,128)(2,1)} %amps.1, bf16[3,96,128,128]{3,2,1,0:T(8,128)(2,1)} %integrals.1), custom_call_target="tpu_custom_call" | custom-call | tf_op jit(solution)/shard_map/ladder/pallas_call | solution.py:371
  37.7 1.0 %reshape.6 = f32[4,2,2,4,2,4,16]{6,5,4,3,2,1,0:T(4,128)S(1)} reshape(f32[4,2,8,128]{3,2,1,0:T(8,128)} %ladder.1) | data formatting | bytes 65536 | tf_op jit(solution)/shard_map/reshape | solution.py:413
  38.7 0.1 reshape.7
  38.8 0.7 %copy.6 = f32[16,3,96]{2,0,1:T(8,128)} copy(f32[16,3,96]{0,2,1:T(8,128)S(1)} %reshape.7) | data formatting | bytes 36864 | tf_op jit(solution)/shard_map/reshape | solution.py:414
  (1 shorter events, 0.0 us)

commit v7 on v6

--- a/solution.py
+++ b/solution.py
@@ -193,8 +193,6 @@
         term = term.reshape(OWN * WIR, 2, 8, 256)
         acc[second] += jnp.where(low_half[None], term[:, 0], term[:, 1])
 
-    fetch.wait()
-    tile(0, 0)
     relay(1, 0)
     relay(3, 0)
     relay(0, 1)
@@ -202,19 +200,20 @@
     from_partner(2, (1,))
     for i in range(1, 4):
         pl.semaphore_signal(token, inc=1, device_id=(ab, cd ^ i), device_id_type=MESH)
-    rest_arrived(0, 0)
-    rest_arrived(0, 1)
-    for rel, dz in ((0, 1), (0, 3), (1, 0), (3, 0)):
-        tile(rel, dz)
     relay(2, 0, (0,))
     relay(1, 1)
     relay(3, 1)
+    fetch.wait()
+    rest_arrived(0, 0)
+    rest_arrived(0, 1)
+    for rel, dz in ((0, 0), (0, 1), (0, 3), (1, 0), (3, 0)):
+        tile(rel, dz)
+    relay(2, 0, (1,))
     for du in (1, 3):
         for dy in range(2):
             rest_arrived(du, dy)
     for rel, dz in ((1, 1), (1, 3), (3, 1), (3, 3)):
         tile(rel, dz)
-    relay(2, 0, (1,))
 
     to_core = lax.rem(irrep, 2)
 
@@ -228,18 +227,20 @@
             device_id_type=MESH,
         )
 
-    def msg_copy(block, to_high, tile_at):
+    my_tile = (irrep // 2 * 2 + high) * GROUP + slot
+
+    def msg_copy(block, to_high):
         return pltpu.make_async_remote_copy(
             src_ref=msgs.at[block],
-            dst_ref=mirror.at[tile_at],
-            send_sem=msg_send.at[to_high, block],
-            recv_sem=msg_recv.at[tile_at],
+            dst_ref=mirror.at[my_tile],
+            send_sem=msg_send,
+            recv_sem=msg_recv,
             device_id=(block, to_high * 2 + to_core),
             device_id_type=MESH,
         )
 
-    my_tile = (irrep // 2 * 2 + high) * GROUP + slot
-    stays = to_core == core
+    def local_copy():
+        return pltpu.make_async_copy(msgs.at[ab], mirror.at[my_tile], msg_recv)
 
     def own_copy(n, peer, sender):
         return pltpu.make_async_remote_copy(
@@ -284,13 +285,16 @@
         pass_copy(rel // 2, other).wait_recv()
         placed = placed + taken[rel // 2]
         msgs[pl.ds(second * GROUP, GROUP)] = placed[16:].reshape(GROUP, 8, 128)
-        for i in range(GROUP):
-            block = second * GROUP + i
-            for to_high in range(2):
-
-                @pl.when((block != ab) | (to_high * 2 + to_core != cd))
-                def _():
-                    msg_copy(block, to_high, my_tile).start()
+        for dz in (2, 1, 3, 0):
+            for dy in (1, 0):
+                for to_high in (1 - high, high):
+                    block = second * GROUP + along_z[dz] + along_y[dy]
+                    if dz or dy or to_high is not high:
+                        msg_copy(block, to_high).start()
+                        continue
+                    here = (block == ab) & (to_core == core)
+                    pl.when(~here)(msg_copy(block, to_high).start)
+                    pl.when(here)(local_copy().start)
 
         at = second // 2
         own[high, at] = placed[:16].reshape(2, 8, 128)
@@ -308,8 +312,6 @@
     for n in range(2):
         given[n] = passed[:, n * 128 : (n + 1) * 128]
         pass_copy(n, other).start()
-    pl.semaphore_wait(token, 3)
-    finish(0)
     rest_arrived(2, 0, (1,))
     for dv in (1, 3):
         arrived(1, 2, dv, 1)
@@ -317,53 +319,39 @@
         far_arrived(0, du)
     for dz in (0, 1, 3):
         tile(2, dz)
+    pl.semaphore_wait(token, 3)
+    finish(0)
     far_arrived(0, 2)
     far_arrived(1, 2)
     tile(2, 2)
     finish(2)
 
-    @pl.when(stays)
-    def _():
-        mirror[my_tile] = msgs[ab]
-
-    def collect(i, carry):
-        @pl.when((i != my_tile) | ~stays)
-        def _():
-            msg_copy(ab, 0, i).wait_recv()
-
+    def sent_items(i, carry):
+        item_copy(i, 0, ab, ab).wait_send()
         return carry
 
-    lax.fori_loop(0, 32, collect, 0)
+    lax.fori_loop(0, len(sent), sent_items, 0)
+    for n in range(2):
+        pass_copy(n, cd).wait_send()
+
+    pltpu.make_async_copy(msgs, mirror, msg_recv).wait()
     mirrored = jnp.sum(mirror[...].reshape(2, 2, 2, 4, 8, 128), axis=(1, 3))
     for n in range(2):
         own_copy(n, cd, 1 - high).wait_recv()
     halves[core] = (own[0] + own[1]) + mirrored
     half_copy(other, core).start()
+    for n in range(2):
+        own_copy(n, cd, high).wait_send()
     half_copy(cd, 1 - core).wait_recv()
     for second in range(IRREPS):
         out[second] = halves[second % 2, second // 2]
-
-    def sent_items(i, carry):
-        item_copy(i, 0, ab, ab).wait_send()
-        return carry
-
-    def sent_msgs(i, carry):
-        for to_high in range(2):
-            for n in range(2):
-                block = (core + 2 * n) * GROUP + i
-
-                @pl.when((block != ab) | (to_high * 2 + to_core != cd))
-                def _():
-                    msg_copy(block, to_high, my_tile).wait_send()
-
-        return carry
-
-    lax.fori_loop(0, len(sent), sent_items, 0)
-    lax.fori_loop(0, GROUP, sent_msgs, 0)
-    for n in range(2):
-        pass_copy(n, cd).wait_send()
-        own_copy(n, cd, high).wait_send()
     half_copy(cd, core).wait_send()
+    tiles = pltpu.make_async_copy(msgs.at[pl.ds(0, 31)], mirror.at[pl.ds(0, 31)], msg_send)
+    tiles.wait()
+
+    @pl.when(to_core != core)
+    def _():
+        pltpu.make_async_copy(msgs.at[0], mirror.at[0], msg_send).wait()
 
 
 def on_device(integrals, amplitudes, block_sizes):
@@ -397,8 +385,8 @@
             pltpu.SemaphoreType.DMA((2, 32)),
             pltpu.SemaphoreType.DMA((2,)),
             pltpu.SemaphoreType.DMA((2,)),
-            pltpu.SemaphoreType.DMA((2, 32)),
-            pltpu.SemaphoreType.DMA((32,)),
+            pltpu.SemaphoreType.DMA,
+            pltpu.SemaphoreType.DMA,
             pltpu.SemaphoreType.DMA((2,)),
             pltpu.SemaphoreType.DMA((2,)),
             pltpu.SemaphoreType.DMA,

time: 39.7 us -> 38.7 us (0.975)
  Pallas kernels: 37.7 us -> 36.7 us
    pallas_call x1, Pallas kernels: 37.7 us -> 36.7 us  [on_device(): pl.pallas_call(kernel, out_shape=jax.ShapeDtypeStruct((IRREPS, 2, 8, 128)...]
where the time goes in v7:
time: 38.7 us; the launch traced here: 38.5 us
  Pallas kernels  36.7 us (95%)
  local copies, waits for them, and re-layouts  1.76 us (5%)
    pallas_call x1, Pallas kernels, on_device(): pl.pallas_call(kernel, out_shape=jax.ShapeDtypeStruct((IRREPS, 2, 8, 128)...  36.7 us
    reshape x1, local copies, waits for them, and re-layouts, on_device(): packed.reshape(IRREPS, 2, 2, 4, 2, 4, NPAIR)[:, :, :, :OWN, :, :OWN]  0.97 us

profile of v7, /device:TPU:1, one launch (start us, length us, event | category | flops | bytes accessed | tf_op | source)
XLA Modules:
  0.0 38.5 jit_solution(1097400973924283586)
XLA Ops:
  0.0 36.7 %ladder.1 = f32[4,2,8,128]{3,2,1,0:T(8,128)} custom-call(s32[4]{0:T(128)} %sizes.1, bf16[16,16,128]{2,1,0:T(8,128)(2,1)} %amps.1, bf16[3,96,128,128]{3,2,1,0:T(8,128)(2,1)} %integrals.1), custom_call_target="tpu_custom_call" | custom-call | tf_op jit(solution)/shard_map/ladder/pallas_call | solution.py:359
  36.7 1.0 %reshape.6 = f32[4,2,2,4,2,4,16]{6,5,4,3,2,1,0:T(4,128)S(1)} reshape(f32[4,2,8,128]{3,2,1,0:T(8,128)} %ladder.1) | data formatting | bytes 65536 | tf_op jit(solution)/shard_map/reshape | solution.py:401
  37.7 0.1 reshape.7
  37.8 0.7 %copy.6 = f32[16,3,96]{2,0,1:T(8,128)} copy(f32[16,3,96]{0,2,1:T(8,128)S(1)} %reshape.7) | data formatting | bytes 36864 | tf_op jit(solution)/shard_map/reshape | solution.py:402
  (1 shorter events, 0.0 us)

commit v8 on v7

--- a/solution.py
+++ b/solution.py
@@ -28,9 +28,9 @@
 
 
 def kernel(
-    sizes, amps, integrals, out, ints, plain, panels, acc, given, taken, msgs, mirror, own, halves,
-    spread_pairs, keep_rows, gather_rows,
-    ints_sem, plain_sem, send_sem, item_recv, pass_send, pass_recv,
+    sizes_at, amps, integrals, out, sizes, ints, plain, panels, acc, given, taken, msgs, mirror, own, halves,
+    spread_pairs, keep_rows, gather_rows, take_lanes, put_rows, keep_lanes,
+    sizes_sem, ints_sem, plain_sem, send_sem, item_recv, pass_send, pass_recv,
     msg_send, msg_recv, own_send, own_recv, half_send, half_recv, token,
 ):
     ab = lax.axis_index("ab")
@@ -47,6 +47,8 @@
 
     fetch_own = pltpu.make_async_copy(amps, plain, plain_sem)
     fetch_own.start()
+    fetch_sizes = pltpu.make_async_copy(sizes_at, sizes, sizes_sem)
+    fetch_sizes.start()
 
     along_x = [lax.rem(irrep + d, 4) * GROUP for d in range(4)]
     along_z = [lax.rem(ring + d, 4) * 2 for d in range(4)]
@@ -68,6 +70,7 @@
     fetch = pltpu.make_async_copy(integrals, ints, ints_sem)
     fetch.start()
 
+    fetch_sizes.wait()
     row_limit = sizes[irrep] - slot * CB
     col_limit = sizes[cd]
     shape = (NPAIR * CB, BLK)
@@ -144,7 +147,6 @@
     for half in range(2):
         send(half, (0, 0, 0), (2, 0, 0))
 
-    acc[...] = jnp.zeros_like(acc)
     spread_pairs[...] = (
         (iota((512, 128), 1) & 15) == ((iota((512, 128), 0) & 255) >> 4)
     ).astype(BF16)
@@ -165,17 +167,22 @@
     )
     goal = (iota((80, 144), 0) == goal).astype(BF16)
     gather_rows[...] = jnp.concatenate([goal, goal], axis=1)
+    frm = iota((96, 128), 0)
+    take_lanes[...] = (
+        iota((96, 128), 1) == (frm // 48) * 64 + (lax.rem(frm, 48) >> 4) * 16 + (frm & 15)
+    ).astype(BF16)
+    for a in range(OWN):
+        b = iota((64, 128), 1)
+        b_row = lax.rem(b, WIR) // 6
+        b_row = (b // (2 * WIR)) * 16 + (b_row >> 1) * 8 + (b_row & 1) * 4 + a
+        b_here = (((b // WIR) & 1) == core) & (b < IRREPS * WIR)
+        put_rows[:, pl.ds(a * 128, 128)] = (
+            ((iota((64, 128), 0) & 31) == b_row) & b_here
+        ).astype(BF16)
+    frm = iota((96, 128), 0)
+    keep_lanes[...] = ((frm >> 4) == lax.rem(iota((96, 128), 1), 6)).astype(F32)
     diagonal = (iota((8, 256), 1) & 7) == iota((8, 256), 0)
     low_half = (iota((8, 256), 1) & 15) < 8
-
-    first_ring(1)
-    first_ring(3)
-    from_partner(0)
-    relay(0, 0)
-    first_ring(2, (0,))
-    from_partner(1)
-    from_partner(3)
-    from_partner(2, (0,))
 
     def tile(rel, dz):
         source = irrep ^ rel
@@ -191,24 +198,32 @@
         left = left.reshape(OWN * WIR * CB, 256)
         term = jnp.dot(left, weights, preferred_element_type=F32)
         term = term.reshape(OWN * WIR, 2, 8, 256)
-        acc[second] += jnp.where(low_half[None], term[:, 0], term[:, 1])
-
+        term = jnp.where(low_half[None], term[:, 0], term[:, 1])
+        if dz:
+            term = acc[second] + term
+        acc[second] = term
+
+    first_ring(1)
+    first_ring(3)
+    from_partner(0)
+    relay(0, 0)
+    first_ring(2)
+    from_partner(1)
+    from_partner(3)
+    fetch.wait()
     relay(1, 0)
     relay(3, 0)
     relay(0, 1)
-    first_ring(2, (1,))
-    from_partner(2, (1,))
+    from_partner(2)
     for i in range(1, 4):
         pl.semaphore_signal(token, inc=1, device_id=(ab, cd ^ i), device_id_type=MESH)
-    relay(2, 0, (0,))
+    relay(2, 0)
     relay(1, 1)
     relay(3, 1)
-    fetch.wait()
     rest_arrived(0, 0)
     rest_arrived(0, 1)
     for rel, dz in ((0, 0), (0, 1), (0, 3), (1, 0), (3, 0)):
         tile(rel, dz)
-    relay(2, 0, (1,))
     for du in (1, 3):
         for dy in range(2):
             rest_arrived(du, dy)
@@ -279,9 +294,8 @@
             gather_rows[...], split2(jnp.concatenate(kept, axis=1), 0), preferred_element_type=F32
         )
 
-    def finish(rel):
+    def finish(rel, placed):
         second = rel ^ cd
-        placed = ending(rel)
         pass_copy(rel // 2, other).wait_recv()
         placed = placed + taken[rel // 2]
         msgs[pl.ds(second * GROUP, GROUP)] = placed[16:].reshape(GROUP, 8, 128)
@@ -319,12 +333,13 @@
         far_arrived(0, du)
     for dz in (0, 1, 3):
         tile(2, dz)
-    pl.semaphore_wait(token, 3)
-    finish(0)
     far_arrived(0, 2)
     far_arrived(1, 2)
     tile(2, 2)
-    finish(2)
+    pl.semaphore_wait(token, 3)
+    placed = ending(2, 0)
+    finish(2, placed[:, :128])
+    finish(0, placed[:, 128:])
 
     def sent_items(i, carry):
         item_copy(i, 0, ab, ab).wait_send()
@@ -338,13 +353,19 @@
     mirrored = jnp.sum(mirror[...].reshape(2, 2, 2, 4, 8, 128), axis=(1, 3))
     for n in range(2):
         own_copy(n, cd, 1 - high).wait_recv()
-    halves[core] = (own[0] + own[1]) + mirrored
+    total = ((own[0] + own[1]) + mirrored).reshape(32, 128)
+    turned = lax.dot_general(
+        take_lanes[...], split2(total, 0), (((1,), (1,)), ((), ())), preferred_element_type=F32
+    )
+    wide = jnp.dot(turned.astype(BF16), put_rows[...], preferred_element_type=F32)
+    for a in range(OWN):
+        part = wide[:, a * 128 : (a + 1) * 128] * keep_lanes[...]
+        halves[core, a] = jnp.sum(part.reshape(6, NPAIR, 128), axis=0)
     half_copy(other, core).start()
     for n in range(2):
         own_copy(n, cd, high).wait_send()
     half_copy(cd, 1 - core).wait_recv()
-    for second in range(IRREPS):
-        out[second] = halves[second % 2, second // 2]
+    out[...] = (halves[0] + halves[1])[:, :, : IRREPS * WIR]
     half_copy(cd, core).wait_send()
     tiles = pltpu.make_async_copy(msgs.at[pl.ds(0, 31)], mirror.at[pl.ds(0, 31)], msg_send)
     tiles.wait()
@@ -356,16 +377,17 @@
 
 def on_device(integrals, amplitudes, block_sizes):
     vmem = pl.BlockSpec(memory_space=pltpu.VMEM)
-    packed = pl.pallas_call(
+    rows = pl.pallas_call(
         kernel,
-        out_shape=jax.ShapeDtypeStruct((IRREPS, 2, 8, 128), F32),
+        out_shape=jax.ShapeDtypeStruct((OWN, NPAIR, IRREPS * WIR), F32),
         in_specs=[
-            pl.BlockSpec(memory_space=pltpu.SMEM),
-            pl.BlockSpec(memory_space=pl.ANY),
-            pl.BlockSpec(memory_space=pl.ANY),
+            pl.BlockSpec(memory_space=pltpu.HBM),
+            pl.BlockSpec(memory_space=pltpu.HBM),
+            pl.BlockSpec(memory_space=pltpu.HBM),
         ],
         out_specs=vmem,
         scratch_shapes=[
+            pltpu.SMEM((IRREPS,), jnp.int32),
             pltpu.VMEM(integrals.shape, BF16),
             pltpu.VMEM(amplitudes.shape, BF16),
             pltpu.VMEM((2, 32, BLK, NPAIR * CB // 2), BF16),
@@ -375,10 +397,14 @@
             pltpu.VMEM((32, 8, 128), F32),
             pltpu.VMEM((32, 8, 128), F32),
             pltpu.VMEM((2, 2, 2, 8, 128), F32),
-            pltpu.VMEM((2, 2, 2, 8, 128), F32),
+            pltpu.VMEM((2, OWN, NPAIR, 128), F32),
             pltpu.VMEM((512, 128), BF16),
             pltpu.VMEM((144, 128), F32),
             pltpu.VMEM((80, 288), BF16),
+            pltpu.VMEM((96, 128), BF16),
+            pltpu.VMEM((64, OWN * 128), BF16),
+            pltpu.VMEM((96, 128), F32),
+            pltpu.SemaphoreType.DMA,
             pltpu.SemaphoreType.DMA,
             pltpu.SemaphoreType.DMA,
             pltpu.SemaphoreType.DMA((62,)),
@@ -398,8 +424,7 @@
         ),
         name="ladder",
     )(block_sizes, amplitudes, integrals)
-    packed = packed.reshape(IRREPS, 2, 2, 4, 2, 4, NPAIR)[:, :, :, :OWN, :, :OWN]
-    return packed.transpose(6, 3, 0, 1, 2, 4, 5).reshape(NPAIR, OWN, IRREPS * WIR)
+    return rows.transpose(1, 0, 2)
 
 
 def solution(mesh):

time: 38.7 us -> 36.3 us (0.938)
  Pallas kernels: 36.7 us -> 34.8 us
  local copies, waits for them, and re-layouts: 1.76 us -> 1.35 us
    pallas_call x1, Pallas kernels: 36.7 us -> 34.8 us  [on_device(): pl.pallas_call(kernel, out_shape=jax.ShapeDtypeStruct((OWN, NPAIR, IRREPS...]
    reshape x3 -> x0, local copies, waits for them, and re-layouts: 1.74 us -> none  [the longest x1 0.97 us: on_device(): packed.reshape(IRREPS, 2, 2, 4, 2, 4, NPAIR)[:, :, :, :OWN, :, :OWN]]
    unnamed x0 -> x1, local copies, waits for them, and re-layouts: none -> 1.35 us
where the time goes in v8:
time: 36.3 us; the launch traced here: 36.1 us
  Pallas kernels  34.8 us (96%)
  local copies, waits for them, and re-layouts  1.35 us (4%)
    pallas_call x1, Pallas kernels, on_device(): pl.pallas_call(kernel, out_shape=jax.ShapeDtypeStruct((OWN, NPAIR, IRREPS...  34.8 us
    unnamed x1, local copies, waits for them, and re-layouts  1.35 us

profile of v8, /device:TPU:1, one launch (start us, length us, event | category | flops | bytes accessed | tf_op | source)
XLA Modules:
  0.0 36.1 jit_solution(17234155518631468838)
XLA Ops:
  0.0 34.8 %ladder.1 = f32[3,16,96]{2,1,0:T(8,128)} custom-call(s32[4]{0:T(128)} %sizes_at.1, bf16[16,16,128]{2,1,0:T(8,128)(2,1)} %amps.1, bf16[3,96,128,128]{3,2,1,0:T(8,128)(2,1)} %integrals.1), custom_call_target="tpu_custom_call" | custom-call | tf_op jit(solution)/shard_map/ladder/pallas_call | solution.py:380
  34.8 1.3 %copy.5 = f32[16,3,96]{2,0,1:T(8,128)} copy(f32[16,3,96]{2,0,1:T(8,128)} %bitcast.1) | data formatting | bytes 36864

commit v9 on v8

--- a/solution.py
+++ b/solution.py
@@ -118,7 +118,7 @@
             arrived(half, du, 0, 1)
             onward(half, du, 1)
 
-    from_below = ((0, 0), (2, 0), (1, 1), (3, 1))
+    from_below = ((0, 0), (1, 0), (3, 1))
 
     def relay(du, dy, halves=both):
         dv = 3 if (du, dy) in from_below else 1
@@ -131,8 +131,13 @@
         for half in halves:
             arrived(half, du, dv, dy)
 
+    def far_to_partner(du):
+        for half in range(2):
+            arrived(half, du, 2, 0)
+            send(half, (du, 2, 0), (0, 0, 1))
+
     def far_arrived(half, du):
-        for dy in range(2):
+        for dy in range(1 if du == 0 else 0, 2):
             arrived(half, du, 2, dy)
 
     pl.semaphore_wait(barrier, 10)
@@ -213,15 +218,17 @@
     fetch.wait()
     relay(1, 0)
     relay(3, 0)
-    relay(0, 1)
     from_partner(2)
     for i in range(1, 4):
         pl.semaphore_signal(token, inc=1, device_id=(ab, cd ^ i), device_id_type=MESH)
     relay(2, 0)
     relay(1, 1)
     relay(3, 1)
+    far_to_partner(0)
     rest_arrived(0, 0)
-    rest_arrived(0, 1)
+    for half in range(2):
+        arrived(half, 0, 1, 1)
+        arrived(half, 0, 3, 1)
     for rel, dz in ((0, 0), (0, 1), (0, 3), (1, 0), (3, 0)):
         tile(rel, dz)
     for du in (1, 3):
@@ -420,10 +427,15 @@
             pltpu.SemaphoreType.REGULAR,
         ],
         compiler_params=pltpu.CompilerParams(
-            collective_id=0, has_side_effects=True, vmem_limit_bytes=56 << 20
+            collective_id=0, has_side_effects=True, vmem_limit_bytes=50 << 20
         ),
         name="ladder",
-    )(block_sizes, amplitudes, integrals)
+    )(
+        *(
+            pltpu.with_memory_space_constraint(x, pltpu.HBM)
+            for x in (block_sizes, amplitudes, integrals)
+        )
+    )
     return rows.transpose(1, 0, 2)
 
 

time: 36.3 us -> 34.8 us (0.959)
  local copies, waits for them, and re-layouts: 1.35 us -> 0.61 us
  Pallas kernels: 34.8 us -> 34.1 us
    unnamed x1, local copies, waits for them, and re-layouts: 1.35 us -> 0.61 us
    pallas_call x1, Pallas kernels: 34.8 us -> 34.1 us  [on_device(): pl.pallas_call(kernel, out_shape=jax.ShapeDtypeStruct((OWN, NPAIR, IRREPS...]
where the time goes in v9:
time: 34.8 us; the launch traced here: 34.7 us
  Pallas kernels  34.1 us (98%)
  local copies, waits for them, and re-layouts  0.61 us (2%)
    pallas_call x1, Pallas kernels, on_device(): pl.pallas_call(kernel, out_shape=jax.ShapeDtypeStruct((OWN, NPAIR, IRREPS...  34.1 us

profile of v9, /device:TPU:1, one launch (start us, length us, event | category | flops | bytes accessed | tf_op | source)
XLA Modules:
  0.0 34.7 jit_solution(17721715783755363458)
XLA Ops:
  0.0 34.1 %ladder.1 = f32[3,16,96]{2,1,0:T(8,128)S(1)} custom-call(s32[4]{0:T(128)} %sizes_at.1, bf16[16,16,128]{2,1,0:T(8,128)(2,1)} %amps.1, bf16[3,96,128,128]{3,2,1,0:T(8,128)(2,1)} %integrals.1), custom_call_target="tpu_custom_call" | custom-call | tf_op jit(solution)/shard_map/ladder/pallas_call | solution.py:387
  34.1 0.6 %copy.5 = f32[16,3,96]{2,0,1:T(8,128)} copy(f32[16,3,96]{2,0,1:T(8,128)S(1)} %bitcast.1) | data formatting | bytes 36864

commit v10 on v9

--- a/solution.py
+++ b/solution.py
@@ -102,7 +102,7 @@
     def onward(half, du, dy):
         send(half, (du, 0, dy), (0, 1, 0))
         send(half, (du, 0, dy), (0, 3, 0))
-        if (du, dy) == (2, 1):
+        if dy:
             send(half, (du, 0, dy), (0, 2, 0))
 
     both = (0, 1)
@@ -118,7 +118,7 @@
             arrived(half, du, 0, 1)
             onward(half, du, 1)
 
-    from_below = ((0, 0), (1, 0), (3, 1))
+    from_below = ((0, 0), (1, 0))
 
     def relay(du, dy, halves=both):
         dv = 3 if (du, dy) in from_below else 1
@@ -131,13 +131,8 @@
         for half in halves:
             arrived(half, du, dv, dy)
 
-    def far_to_partner(du):
-        for half in range(2):
-            arrived(half, du, 2, 0)
-            send(half, (du, 2, 0), (0, 0, 1))
-
     def far_arrived(half, du):
-        for dy in range(1 if du == 0 else 0, 2):
+        for dy in range(2):
             arrived(half, du, 2, dy)
 
     pl.semaphore_wait(barrier, 10)
@@ -222,9 +217,6 @@
     for i in range(1, 4):
         pl.semaphore_signal(token, inc=1, device_id=(ab, cd ^ i), device_id_type=MESH)
     relay(2, 0)
-    relay(1, 1)
-    relay(3, 1)
-    far_to_partner(0)
     rest_arrived(0, 0)
     for half in range(2):
         arrived(half, 0, 1, 1)
@@ -232,8 +224,10 @@
     for rel, dz in ((0, 0), (0, 1), (0, 3), (1, 0), (3, 0)):
         tile(rel, dz)
     for du in (1, 3):
-        for dy in range(2):
-            rest_arrived(du, dy)
+        rest_arrived(du, 0)
+        for half in range(2):
+            for dv in (1, 3):
+                arrived(half, du, dv, 1)
     for rel, dz in ((1, 1), (1, 3), (3, 1), (3, 3)):
         tile(rel, dz)
 

time: 34.8 us -> 33.7 us (0.968)
  Pallas kernels: 34.1 us -> 33 us
    pallas_call x1, Pallas kernels: 34.1 us -> 33 us  [on_device(): pl.pallas_call(kernel, out_shape=jax.ShapeDtypeStruct((OWN, NPAIR, IRREPS...]
where the time goes in v10:
time: 33.7 us; the launch traced here: 33.6 us
  Pallas kernels  33 us (98%)
  local copies, waits for them, and re-layouts  0.61 us (2%)
    pallas_call x1, Pallas kernels, on_device(): pl.pallas_call(kernel, out_shape=jax.ShapeDtypeStruct((OWN, NPAIR, IRREPS...  33 us

profile of v10, /device:TPU:1, one launch (start us, length us, event | category | flops | bytes accessed | tf_op | source)
XLA Modules:
  0.0 33.6 jit_solution(17313604976647407299)
XLA Ops:
  0.0 33.0 %ladder.1 = f32[3,16,96]{2,1,0:T(8,128)S(1)} custom-call(s32[4]{0:T(128)} %sizes_at.1, bf16[16,16,128]{2,1,0:T(8,128)(2,1)} %amps.1, bf16[3,96,128,128]{3,2,1,0:T(8,128)(2,1)} %integrals.1), custom_call_target="tpu_custom_call" | custom-call | tf_op jit(solution)/shard_map/ladder/pallas_call | solution.py:381
  33.0 0.6 %copy.5 = f32[16,3,96]{2,0,1:T(8,128)} copy(f32[16,3,96]{2,0,1:T(8,128)S(1)} %bitcast.1) | data formatting | bytes 36864

commit v11 on v10

--- a/solution.py
+++ b/solution.py
@@ -60,7 +60,7 @@
         return along_x[du] + along_z[dv] + along_y[dy]
 
     barrier = pltpu.get_barrier_semaphore()
-    for du, dv, dy in ((1, 0, 0), (3, 0, 0), (2, 0, 0), (0, 1, 0), (0, 3, 0), (0, 2, 0), (0, 0, 1)):
+    for du, dv, dy in ((2, 0, 0), (0, 2, 0), (1, 0, 0), (3, 0, 0), (0, 1, 0), (0, 3, 0), (0, 0, 1)):
         pl.semaphore_signal(
             barrier, inc=1, device_id=(place(0, du, dv, dy), cd), device_id_type=MESH
         )
@@ -299,6 +299,9 @@
         second = rel ^ cd
         pass_copy(rel // 2, other).wait_recv()
         placed = placed + taken[rel // 2]
+        at = second // 2
+        own[high, at] = placed[:16].reshape(2, 8, 128)
+        own_copy(at, cd ^ 2, high).start()
         msgs[pl.ds(second * GROUP, GROUP)] = placed[16:].reshape(GROUP, 8, 128)
         for dz in (2, 1, 3, 0):
             for dy in (1, 0):
@@ -311,9 +314,6 @@
                     pl.when(~here)(msg_copy(block, to_high).start)
                     pl.when(here)(local_copy().start)
 
-        at = second // 2
-        own[high, at] = placed[:16].reshape(2, 8, 128)
-        own_copy(at, cd ^ 2, high).start()
 
     far_arrived(1, 0)
     rest_arrived(2, 0, (0,))
@@ -321,7 +321,7 @@
         arrived(0, 2, dv, 1)
     far_arrived(1, 1)
     far_arrived(1, 3)
-    for rel, dz in ((1, 2), (3, 2), (0, 2)):
+    for rel, dz in ((1, 2), (3, 2)):
         tile(rel, dz)
     passed = ending(1, 3)
     for n in range(2):
@@ -332,6 +332,7 @@
         arrived(1, 2, dv, 1)
     for du in (0, 1, 3):
         far_arrived(0, du)
+    tile(0, 2)
     for dz in (0, 1, 3):
         tile(2, dz)
     far_arrived(0, 2)
@@ -365,15 +366,16 @@
     half_copy(other, core).start()
     for n in range(2):
         own_copy(n, cd, high).wait_send()
+    tiles = pltpu.make_async_copy(msgs.at[pl.ds(0, 31)], mirror.at[pl.ds(0, 31)], msg_send)
+    tiles.wait()
+
+    @pl.when(to_core != core)
+    def _():
+        pltpu.make_async_copy(msgs.at[0], mirror.at[0], msg_send).wait()
+
     half_copy(cd, 1 - core).wait_recv()
     out[...] = (halves[0] + halves[1])[:, :, : IRREPS * WIR]
     half_copy(cd, core).wait_send()
-    tiles = pltpu.make_async_copy(msgs.at[pl.ds(0, 31)], mirror.at[pl.ds(0, 31)], msg_send)
-    tiles.wait()
-
-    @pl.when(to_core != core)
-    def _():
-        pltpu.make_async_copy(msgs.at[0], mirror.at[0], msg_send).wait()
 
 
 def on_device(integrals, amplitudes, block_sizes):

time: 33.7 us -> 33.5 us (level)
  no operation moved by 1% of the time
where the time goes in v11:
time: 33.5 us; the launch traced here: 33.4 us
  Pallas kernels  32.8 us (98%)
  local copies, waits for them, and re-layouts  0.61 us (2%)
    pallas_call x1, Pallas kernels, on_device(): pl.pallas_call(kernel, out_shape=jax.ShapeDtypeStruct((OWN, NPAIR, IRREPS...  32.8 us

profile of v11, /device:TPU:1, one launch (start us, length us, event | category | flops | bytes accessed | tf_op | source)
XLA Modules:
  0.0 33.4 jit_solution(9264846791199634642)
XLA Ops:
  0.0 32.8 %ladder.1 = f32[3,16,96]{2,1,0:T(8,128)S(1)} custom-call(s32[4]{0:T(128)} %sizes_at.1, bf16[16,16,128]{2,1,0:T(8,128)(2,1)} %amps.1, bf16[3,96,128,128]{3,2,1,0:T(8,128)(2,1)} %integrals.1), custom_call_target="tpu_custom_call" | custom-call | tf_op jit(solution)/shard_map/ladder/pallas_call | solution.py:383
  32.8 0.6 %copy.5 = f32[16,3,96]{2,0,1:T(8,128)} copy(f32[16,3,96]{2,0,1:T(8,128)S(1)} %bitcast.1) | data formatting | bytes 36864

commit v12 on v11

--- a/solution.py
+++ b/solution.py
@@ -216,13 +216,13 @@
     from_partner(2)
     for i in range(1, 4):
         pl.semaphore_signal(token, inc=1, device_id=(ab, cd ^ i), device_id_type=MESH)
-    relay(2, 0)
     rest_arrived(0, 0)
     for half in range(2):
         arrived(half, 0, 1, 1)
         arrived(half, 0, 3, 1)
     for rel, dz in ((0, 0), (0, 1), (0, 3), (1, 0), (3, 0)):
         tile(rel, dz)
+    relay(2, 0)
     for du in (1, 3):
         rest_arrived(du, 0)
         for half in range(2):

time: 33.5 us -> 33.5 us (level)
  no operation moved by 1% of the time
where the time goes in v12:
time: 33.5 us; the launch traced here: 33.4 us
  Pallas kernels  32.8 us (98%)
  local copies, waits for them, and re-layouts  0.61 us (2%)
    pallas_call x1, Pallas kernels, on_device(): pl.pallas_call(kernel, out_shape=jax.ShapeDtypeStruct((OWN, NPAIR, IRREPS...  32.8 us

profile of v12, /device:TPU:1, one launch (start us, length us, event | category | flops | bytes accessed | tf_op | source)
XLA Modules:
  0.0 33.4 jit_solution(1395057899183543470)
XLA Ops:
  0.0 32.8 %ladder.1 = f32[3,16,96]{2,1,0:T(8,128)S(1)} custom-call(s32[4]{0:T(128)} %sizes_at.1, bf16[16,16,128]{2,1,0:T(8,128)(2,1)} %amps.1, bf16[3,96,128,128]{3,2,1,0:T(8,128)(2,1)} %integrals.1), custom_call_target="tpu_custom_call" | custom-call | tf_op jit(solution)/shard_map/ladder/pallas_call | solution.py:383
  32.8 0.6 %copy.5 = f32[16,3,96]{2,0,1:T(8,128)} copy(f32[16,3,96]{2,0,1:T(8,128)S(1)} %bitcast.1) | data formatting | bytes 36864
